TPU v7x, 128 devices: a whole 4x4x4 slice. The times are simulated.
128 devices in a mesh: depth: 16 (over z, y_lo, core), height: 8 (over x, y_hi).
Axes of the slice: x: 4, y: 4 (y_hi: 2, y_lo: 2; y = y_hi * 2 + y_lo), z: 4, core: 2. Of those that a mesh axis runs over, the one named last changes fastest.
Arguments:
- volume: bfloat16 [16, 256, 64, 256], P(None, 'depth', 'height'), may hold values from -6 to 6
- kernel: bfloat16 [3, 3, 32, 48], replicated, may hold values from -0.3125 to 0.3125
- conv_bias: float32 [32], replicated, may hold values from -3 to 3
- cotangent: bfloat16 [32, 128, 32, 128], P(None, 'depth', 'height'), may hold values from -6 to 6
Outputs:
- pooled: bfloat16 [32, 128, 32, 128], P(None, ('depth', 'height'))
- grad_volume: bfloat16 [16, 256, 64, 256], P(None, 'depth', 'height')
- grad_kernel: float32 [3, 3, 32, 48], replicated
- grad_bias: float32 [32], replicated
All inputs are finite; a program needn't handle non-finite values.
Results may differ from a plain program's by a relative error of at most 0.005.
Values may be sent and summed in bfloat16 or wider, within the bound.
A program may use at most 128 MiB of HBM per device.

v0:
```python
import math

import jax
import jax.numpy as jnp
from jax import lax
from jax.sharding import PartitionSpec as P

leak_rate = 0.3


def with_halo(block, sides, width):
    for axis, dim in sides:
        count = lax.axis_size(axis)
        forward = [(i, i + 1) for i in range(count - 1)]
        backward = [(target, source) for source, target in forward]
        low = lax.ppermute(
            lax.slice_in_dim(block, block.shape[dim] - width, None, axis=dim), axis, forward
        )
        high = lax.ppermute(lax.slice_in_dim(block, 0, width, axis=dim), axis, backward)
        block = jnp.concatenate([low, block, high], axis=dim)
    return block


def smooth_leaky(values):
    return leak_rate * values + (1.0 - leak_rate) * jax.nn.softplus(values)


def leaky_slope(values):
    return leak_rate + (1.0 - leak_rate) * jax.nn.sigmoid(values)


def pool_cells(tensor):
    channels, depth_n, height_n, width_n = tensor.shape
    return tensor.reshape(channels, depth_n // 2, 2, height_n // 2, 2, width_n // 2, 2).mean(
        axis=(2, 4, 6)
    )


def spread_cells(tensor):
    channels, depth_n, height_n, width_n = tensor.shape
    enlarged = jnp.broadcast_to(
        tensor[:, :, None, :, None, :, None], (channels, depth_n, 2, height_n, 2, width_n, 2)
    )
    return enlarged.reshape(channels, 2 * depth_n, 2 * height_n, 2 * width_n)


def pad_width(tensor):
    return jnp.pad(tensor, ((0, 0), (0, 0), (0, 0), (1, 1)))


def stack_taps(padded):
    width_n = padded.shape[3] - 2
    return jnp.concatenate(
        [padded[..., 0:width_n], padded[..., 1 : width_n + 1], padded[..., 2 : width_n + 2]], axis=0
    )


def shards(volume, kernel, conv_bias, cotangent):
    in_chan, depth_n, height_n, width_n = volume.shape
    out_chan = kernel.shape[2]
    rim_width = 1
    padded = with_halo(volume, (("depth", 1), ("height", 2)), rim_width)
    tap_stack = stack_taps(pad_width(padded))
    out_depth = depth_n + 2 * rim_width - 2
    out_height = height_n + 2 * rim_width - 2
    summed = jnp.zeros((out_chan, out_depth, out_height, width_n), jnp.float32)
    for row_tap in range(3):
        for col_tap in range(3):
            window = tap_stack[:, row_tap : row_tap + out_depth, col_tap : col_tap + out_height, :]
            summed = summed + jnp.einsum(
                "ok,kdhw->odhw",
                kernel[row_tap, col_tap],
                window,
                preferred_element_type=jnp.float32,
            )
    before_ext = summed + conv_bias[:, None, None, None]
    rim_offset = rim_width - 1
    pooled = pool_cells(smooth_leaky(before_ext)).astype(jnp.bfloat16)
    relaid = lax.all_to_all(pooled, "height", split_axis=1, concat_axis=2, tiled=True)
    upward = spread_cells(cotangent.astype(jnp.float32)) * 0.125
    inner_grad = (upward * leaky_slope(before_ext)).astype(jnp.bfloat16)
    grad_pad = with_halo(inner_grad, (("depth", 1), ("height", 2)), 1)
    local_grad = grad_pad[:, 1:-1, 1:-1, :]
    grad_taps = stack_taps(pad_width(grad_pad))
    flipped = kernel.reshape(3, 3, out_chan, 3, in_chan)[:, :, :, ::-1, :]
    back_kernel = flipped.transpose(0, 1, 3, 2, 4).reshape(3, 3, 3 * out_chan, in_chan)
    gathered = jnp.zeros((in_chan, depth_n, height_n, width_n), jnp.float32)
    kernel_rows = []
    for row_tap in range(3):
        kernel_cols = []
        for col_tap in range(3):
            window = grad_taps[
                :, 2 - row_tap : 2 - row_tap + depth_n, 2 - col_tap : 2 - col_tap + height_n, :
            ]
            gathered = gathered + jnp.einsum(
                "kc,kdhw->cdhw",
                back_kernel[row_tap, col_tap],
                window,
                preferred_element_type=jnp.float32,
            )
            source = tap_stack[
                :,
                rim_offset + row_tap : rim_offset + row_tap + depth_n,
                rim_offset + col_tap : rim_offset + col_tap + height_n,
                :,
            ]
            kernel_cols.append(
                jnp.einsum("odhw,kdhw->ok", local_grad, source, preferred_element_type=jnp.float32)
            )
        kernel_rows.append(jnp.stack(kernel_cols, axis=0))
    kernel_local = jnp.stack(kernel_rows, axis=0)
    bias_local = jnp.sum(local_grad.astype(jnp.float32), axis=(1, 2, 3))
    kernel_total, bias_total = lax.psum((kernel_local, bias_local), ("depth", "height"))
    voxel_count = depth_n * height_n * width_n * lax.axis_size("depth") * lax.axis_size("height")
    norm_factor = 1.0 / math.sqrt(float(voxel_count))
    return (
        relaid,
        gathered.astype(jnp.bfloat16),
        kernel_total * norm_factor,
        bias_total * norm_factor,
    )


def solution(mesh):
    in_specs = (P(None, "depth", "height", None), P(), P(), P(None, "depth", "height", None))
    out_specs = (
        P(None, ("depth", "height"), None, None),
        P(None, "depth", "height", None),
        P(),
        P(),
    )
    return jax.shard_map(shards, mesh=mesh, in_specs=in_specs, out_specs=out_specs, check_vma=False)
```

profile of v0, /device:TPU:1, one launch (start us, length us, event | category | flops | bytes accessed | tf_op | source)
XLA Modules:
  0.0 244.1 jit_solution(8115841605589583685)
XLA Ops:
  0.6 0.9 fusion.134
  1.5 4.6 %collective-permute-start = (bf16[16,1,8,256]{3,0,2,1:T(8,128)(2,1)S(1)}, bf16[16,1,8,256]{3,0,2,1:T(8,128)(2,1)S(1)}, u32[]{:S(2)}, u32[]{:S(2)}) collective-permute-start(bf16[16,1,8,256]{3,0,2,1:T(8,128)(2,1)S(1)} %copy.88), channel_id=1, source_target_pairs={{0,8},{8,16},{16,24},{24,32},{32,40},{40,48},{48,56},{56,64},{64,7... | collective-permute-start | bytes 196616 | tf_op jit(solution)/shard_map/ppermute | solution.py:16
  6.2 1.9 collective-permute-start.1
  8.1 1.8 constant_dynamic-update-slice_fusion.1
  9.9 1.8 collective-permute-done.1
  11.8 0.7 fusion.133
  12.5 1.3 collective-permute-start.3
  13.8 6.2 %collective-permute-start.2 = (bf16[16,18,1,256]{3,0,2,1:T(8,128)(2,1)}, bf16[16,18,1,256]{3,0,2,1:T(8,128)(2,1)}, u32[]{:S(2)}, u32[]{:S(2)}) collective-permute-start(bf16[16,18,1,256]{3,0,2,1:T(8,128)(2,1)} %get-tuple-element.37), channel_id=1, source_target_pairs={{0,1},{1,2},{2,3},{3,4},{4,5},{5,6},{6,7},{8,9},{9,10},{10,11},{11... | collective-permute-start | bytes 442376 | tf_op jit(solution)/shard_map/ppermute | solution.py:16
  19.9 1.8 convert_multiply_fusion
  21.7 1.7 copy.53
  23.4 6.1 %broadcast_in_dim.2 = f32[32,8,2,4,2,128,2]{0,6,5,4,3,2,1:T(2,128)} broadcast(f32[32,8,4,128]{0,3,2,1:T(8,128)S(1)} %copy.53), dimensions={0,1,3,5} | broadcast | bytes 4718592 | tf_op jit(solution)/shard_map/broadcast_in_dim | solution.py:41
  29.5 11.4 %copy.54 = f32[32,16,8,256]{3,0,2,1:T(8,128)} copy(f32[32,16,8,256]{0,3,2,1:T(8,128)} %bitcast.244) | data formatting | bytes 8388608 | tf_op jit(solution)/shard_map/mul | solution.py:80
  41.0 0.1 copy.55
  41.3 2.4 fusion.78
  43.8 0.8 fusion.131
  44.6 1.3 pad_maximum_fusion.1
  45.9 2.6 %fusion.44 = f32[16,8,256,32]{2,3,1,0:T(8,128)} fusion(bf16[48,18,10,256]{3,0,2,1:T(8,128)(2,1)S(1)} %pad_maximum_fusion.1, bf16[3,3,32,48]{3,2,1,0:T(8,128)(2,1)S(1)} %copy-done), kind=kOutput, calls=%fused_computation.59 | convolution fusion | flops 100663296 | bytes 7348224 | tf_op jit(solution)/shard_map/ok,kdhw->odhw/dot_general | solution.py:70
  48.5 2.6 %fusion.48 = f32[16,8,256,32]{2,3,1,0:T(8,128)} fusion(bf16[48,18,10,256]{3,0,2,1:T(8,128)(2,1)S(1)} %pad_maximum_fusion.1, bf16[3,3,32,48]{3,2,1,0:T(8,128)(2,1)S(1)} %copy-done), kind=kOutput, calls=%fused_computation.63 | convolution fusion | flops 100663296 | bytes 7348224 | tf_op jit(solution)/shard_map/ok,kdhw->odhw/dot_general | solution.py:70
  51.2 2.6 %fusion.52 = f32[16,8,256,32]{2,3,1,0:T(8,128)} fusion(bf16[48,18,10,256]{3,0,2,1:T(8,128)(2,1)S(1)} %pad_maximum_fusion.1, bf16[3,3,32,48]{3,2,1,0:T(8,128)(2,1)S(1)} %copy-done), kind=kOutput, calls=%fused_computation.67 | convolution fusion | flops 100663296 | bytes 7348224 | tf_op jit(solution)/shard_map/ok,kdhw->odhw/dot_general | solution.py:70
  53.8 2.6 %fusion.56 = f32[16,8,256,32]{2,3,1,0:T(8,128)} fusion(bf16[48,18,10,256]{3,0,2,1:T(8,128)(2,1)S(1)} %pad_maximum_fusion.1, bf16[3,3,32,48]{3,2,1,0:T(8,128)(2,1)S(1)} %copy-done), kind=kOutput, calls=%fused_computation.71 | convolution fusion | flops 100663296 | bytes 7348224 | tf_op jit(solution)/shard_map/ok,kdhw->odhw/dot_general | solution.py:70
  56.4 2.6 %fusion.60 = f32[16,8,256,32]{2,3,1,0:T(8,128)} fusion(bf16[48,18,10,256]{3,0,2,1:T(8,128)(2,1)S(1)} %pad_maximum_fusion.1, bf16[3,3,32,48]{3,2,1,0:T(8,128)(2,1)S(1)} %copy-done), kind=kOutput, calls=%fused_computation.75 | convolution fusion | flops 100663296 | bytes 7348224 | tf_op jit(solution)/shard_map/ok,kdhw->odhw/dot_general | solution.py:70
  59.1 2.6 %fusion.64 = f32[16,8,256,32]{2,3,1,0:T(8,128)} fusion(bf16[48,18,10,256]{3,0,2,1:T(8,128)(2,1)S(1)} %pad_maximum_fusion.1, bf16[3,3,32,48]{3,2,1,0:T(8,128)(2,1)S(1)} %copy-done), kind=kOutput, calls=%fused_computation.79 | convolution fusion | flops 100663296 | bytes 7348224 | tf_op jit(solution)/shard_map/ok,kdhw->odhw/dot_general | solution.py:70
  61.7 2.6 %fusion.72 = f32[16,8,256,32]{2,3,1,0:T(8,128)} fusion(bf16[48,18,10,256]{3,0,2,1:T(8,128)(2,1)S(1)} %pad_maximum_fusion.1, bf16[3,3,32,48]{3,2,1,0:T(8,128)(2,1)S(1)} %copy-done), kind=kOutput, calls=%fused_computation.87 | convolution fusion | flops 100663296 | bytes 7348224 | tf_op jit(solution)/shard_map/ok,kdhw->odhw/dot_general | solution.py:70
  64.3 2.8 %fusion.68 = f32[16,8,256,32]{2,3,1,0:T(8,128)} fusion(bf16[48,18,10,256]{3,0,2,1:T(8,128)(2,1)S(1)} %pad_maximum_fusion.1, bf16[3,3,32,48]{3,2,1,0:T(8,128)(2,1)S(1)} %copy-done), kind=kOutput, calls=%fused_computation.83 | convolution fusion | flops 100663296 | bytes 7348224 | tf_op jit(solution)/shard_map/ok,kdhw->odhw/dot_general | solution.py:70
  67.1 16.8 %convert_reduce_fusion = (f32[32]{0:T(128)S(1)}, bf16[32,16,8,256]{3,0,2,1:T(8,128)(2,1)S(1)}, f32[32,16,8,256]{3,0,2,1:T(8,128)}) fusion(f32[32,16,8,256]{3,0,2,1:T(8,128)} %copy.54, f32[32]{0:T(128)S(1)} %copy-done.1, bf16[48,18,10,256]{3,0,2,1:T(8,128)(2,1)S(1)} %pad_maximum_fusion.1, bf16[3,3,32,48]{3,2,1,0:T(8,128)(2,1)S(1)} %copy-done, ...), kind=kOutput, calls=%fused_computation.51 | convolution fusion | flops 128974816 | bytes 47194752 | tf_op jit(solution)/shard_map/ok,kdhw->odhw/dot_general | solution.py:70
  83.9 0.7 fusion.132
  84.6 0.9 fusion.105
  85.5 0.9 fusion.102
  86.5 0.9 fusion.99
  87.4 0.9 fusion.87
  88.3 0.9 fusion.84
  89.3 0.9 fusion.81
  90.2 0.9 fusion.96
  91.2 0.9 fusion.93
  92.1 0.9 fusion.90
  93.1 10.4 %copy.48 = f32[32,16,8,256]{0,3,2,1:T(8,128)} copy(f32[32,16,8,256]{3,0,2,1:T(8,128)} %get-tuple-element.30) | data formatting | bytes 8388608 | tf_op jit(solution)/shard_map/add | solution.py:25
  103.5 13.1 %reduce_sum.18 = f32[32,8,4,128]{0,3,2,1:T(8,128)} reduce(f32[32,8,2,4,2,128,2]{0,6,5,4,3,2,1:T(2,128)} %bitcast.245, f32[]{:T(128)} %constant.9.clone.1), dimensions={2,4,6}, to_apply=%region_0.1 | reduce | flops 917504 | bytes 4718596 | tf_op jit(solution)/shard_map/reduce_sum | solution.py:34
  116.6 2.3 copy.49
  118.9 0.8 copy.50
  119.7 6.6 %all-to-all-start = ((bf16[32,8,4,128]{3,2,0,1:T(4,128)(2,1)}), bf16[32,8,4,128]{3,2,0,1:T(4,128)(2,1)S(1)}, u32[]{:S(2)}, u32[]{:S(2)}) async-start(bf16[32,8,4,128]{3,2,0,1:T(4,128)(2,1)} %copy.50), calls=%async_computation | async-start | bytes 524288 | tf_op jit(solution)/shard_map/all_to_all | solution.py:79
  126.3 1.9 collective-permute-start.5
  128.3 3.6 %collective-permute-start.4 = (bf16[32,1,8,256]{3,0,2,1:T(8,128)(2,1)}, bf16[32,1,8,256]{3,0,2,1:T(8,128)(2,1)S(1)}, u32[]{:S(2)}, u32[]{:S(2)}) collective-permute-start(bf16[32,1,8,256]{3,0,2,1:T(8,128)(2,1)} %get-tuple-element.35), channel_id=1, source_target_pairs={{0,8},{8,16},{16,24},{24,32},{32,40},{40,48},{48,56},{56,64},{64,7... | collective-permute-start | bytes 393224 | tf_op jit(solution)/shard_map/ppermute | solution.py:16
  132.0 69.5 %all-reduce.2 = (f32[3,3,32,48]{3,2,1,0:T(8,128)S(1)}, f32[32]{0:T(128)S(1)}) all-reduce(f32[3,3,32,48]{3,2,1,0:T(8,128)S(1)} %pad_maximum_fusion.5, f32[32]{0:T(128)S(1)} %get-tuple-element.26), channel_id=1, replica_groups=mesh['depth'=16,'height'=8] {'depth','height'}, use_global_device_ids=true, to_apply=%region_1.2 | all-reduce | flops 13856 | bytes 110848 | tf_op jit(solution)/shard_map/psum | solution.py:113
  201.5 0.9 pad_maximum_fusion.4
  202.4 1.3 collective-permute-start.7
  203.7 5.5 %collective-permute-start.6 = (bf16[32,18,1,256]{3,0,2,1:T(8,128)(2,1)}, bf16[32,18,1,256]{3,0,2,1:T(8,128)(2,1)S(1)}, u32[]{:S(2)}, u32[]{:S(2)}) collective-permute-start(bf16[32,18,1,256]{3,0,2,1:T(8,128)(2,1)} %get-tuple-element.31), channel_id=1, source_target_pairs={{0,1},{1,2},{2,3},{3,4},{4,5},{5,6},{6,7},{8,9},{9,10},{10,11},{11... | collective-permute-start | bytes 884744 | tf_op jit(solution)/shard_map/ppermute | solution.py:16
  209.2 0.5 broadcast_multiply_fusion.1
  209.7 0.7 broadcast_multiply_fusion
  210.5 0.8 copy.57
  211.3 2.5 %collective-permute-done.7 = bf16[32,18,1,256]{3,0,2,1:T(8,128)(2,1)S(1)} collective-permute-done((bf16[32,18,1,256]{3,0,2,1:T(8,128)(2,1)}, bf16[32,18,1,256]{3,0,2,1:T(8,128)(2,1)S(1)}, u32[]{:S(2)}, u32[]{:S(2)}) %collective-permute-start.7) | collective-permute-done | bytes 294944 | tf_op jit(solution)/shard_map/ppermute | solution.py:19
  213.7 6.1 %collective-permute-done.6 = bf16[32,18,1,256]{3,0,2,1:T(8,128)(2,1)S(1)} collective-permute-done((bf16[32,18,1,256]{3,0,2,1:T(8,128)(2,1)}, bf16[32,18,1,256]{3,0,2,1:T(8,128)(2,1)S(1)}, u32[]{:S(2)}, u32[]{:S(2)}) %collective-permute-start.6) | collective-permute-done | bytes 294944 | tf_op jit(solution)/shard_map/ppermute | solution.py:16
  219.8 4.2 %select_maximum_fusion = bf16[32,18,10,258]{3,0,2,1:T(8,128)(2,1)S(1)} fusion(bf16[32,18,1,256]{3,0,2,1:T(8,128)(2,1)S(1)} %collective-permute-done.7, bf16[32,18,1,256]{3,0,2,1:T(8,128)(2,1)S(1)} %collective-permute-done.6, bf16[32,1,8,256]{3,0,2,1:T(8,128)(2,1)S(1)} %collective-permute-done.5, bf16[32,16,8,256]{3,0,2,1:T(8,128)(2,1)S(1)} %get-tuple-element.27, ...), kind=kLoop, calls=%fused_computation.25 | loop fusion | flops 26749440 | bytes 5921280 | tf_op jit(solution)/shard_map/concatenate | solution.py:20
  224.0 1.9 fusion.130
  225.9 3.1 %pad_maximum_fusion = bf16[96,18,10,256]{3,0,2,1:T(8,128)(2,1)S(1)} fusion(bf16[32,18,10,256]{3,0,2,1:T(8,128)(2,1)S(1)} %get-tuple-element.29, bf16[32,18,1,256]{3,0,2,1:T(8,128)(2,1)S(1)} %collective-permute-done.7, bf16[32,1,8,256]{3,0,2,1:T(8,128)(2,1)S(1)} %collective-permute-done.5, bf16[32,16,8,256]{3,0,2,1:T(8,128)(2,1)S(1)} %get-tuple-element.27, ...), kind=kLoop, calls=%fused_computation.3 | loop fusion | flops 61931520 | bytes 17694720 | tf_op jit(solution)/shard_map/concatenate | solution.py:53
  229.0 0.9 fusion.3
  230.0 0.9 fusion.5
  230.9 0.9 fusion.7
  231.8 0.9 fusion.9
  232.8 0.9 fusion.11
  233.7 0.9 fusion.13
  234.7 0.9 fusion.17
  235.6 2.3 fusion.15
  237.9 3.7 %fusion.108 = bf16[16,16,8,256]{3,0,2,1:T(8,128)(2,1)} fusion(f32[16,8,256,16]{2,3,1,0:T(8,128)S(1)} %fusion.3, f32[16,8,256,16]{2,3,1,0:T(8,128)S(1)} %fusion.5, f32[16,8,256,16]{2,3,1,0:T(8,128)S(1)} %fusion.7, f32[16,8,256,16]{2,3,1,0:T(8,128)S(1)} %fusion.9, f32[16,8,256,16]{2,3,1,0:T(8,128)S(1)} %fusion.11, f32[16,8,256,16]{2,3,1,0:T(8,128)S(1)} %fusion.13, ...), kind=kOutput, calls=%fused_computation.104 | convolution fusion | flops 105381888 | bytes 24121344 | tf_op jit(solution)/shard_map/kc,kdhw->cdhw/dot_general | solution.py:95
  241.6 2.5 %copy.58 = bf16[16,16,8,256]{3,2,1,0:T(8,128)(2,1)} copy(bf16[16,16,8,256]{3,0,2,1:T(8,128)(2,1)} %fusion.108) | data formatting | bytes 2097152
  (22 shorter events, 0.4 us)
Async XLA Ops:
  1.5 6.6 %collective-permute-start = (bf16[16,1,8,256]{3,0,2,1:T(8,128)(2,1)S(1)}, bf16[16,1,8,256]{3,0,2,1:T(8,128)(2,1)S(1)}, u32[]{:S(2)}, u32[]{:S(2)}) collective-permute-start(bf16[16,1,8,256]{3,0,2,1:T(8,128)(2,1)S(1)} %copy.88), channel_id=1, source_target_pairs={{0,8},{8,16},{16,24},{24,32},{32,40},{40,48},{48,56},{56,64},{64,7... | collective-permute-start | bytes 196616 | tf_op jit(solution)/shard_map/ppermute | solution.py:16
  6.2 5.6 %collective-permute-start.1 = (bf16[16,1,8,256]{3,0,2,1:T(8,128)(2,1)S(1)}, bf16[16,1,8,256]{3,0,2,1:T(8,128)(2,1)S(1)}, u32[]{:S(2)}, u32[]{:S(2)}) collective-permute-start(bf16[16,1,8,256]{3,0,2,1:T(8,128)(2,1)S(1)} %copy.89), channel_id=1, source_target_pairs={{8,0},{16,8},{24,16},{32,24},{40,32},{48,40},{56,48},{64,56},{72,6... | collective-permute-start | bytes 196616 | tf_op jit(solution)/shard_map/ppermute | solution.py:19
  12.5 28.8 %collective-permute-start.3 = (bf16[16,18,1,256]{3,0,2,1:T(8,128)(2,1)}, bf16[16,18,1,256]{3,0,2,1:T(8,128)(2,1)S(1)}, u32[]{:S(2)}, u32[]{:S(2)}) collective-permute-start(bf16[16,18,1,256]{3,0,2,1:T(8,128)(2,1)} %get-tuple-element.38), channel_id=1, source_target_pairs={{1,0},{2,1},{3,2},{4,3},{5,4},{6,5},{7,6},{9,8},{10,9},{11,10},{12... | collective-permute-start | bytes 442376 | tf_op jit(solution)/shard_map/ppermute | solution.py:19
  13.8 27.5 %collective-permute-start.2 = (bf16[16,18,1,256]{3,0,2,1:T(8,128)(2,1)}, bf16[16,18,1,256]{3,0,2,1:T(8,128)(2,1)}, u32[]{:S(2)}, u32[]{:S(2)}) collective-permute-start(bf16[16,18,1,256]{3,0,2,1:T(8,128)(2,1)} %get-tuple-element.37), channel_id=1, source_target_pairs={{0,1},{1,2},{2,3},{3,4},{4,5},{5,6},{6,7},{8,9},{9,10},{10,11},{11... | collective-permute-start | bytes 442376 | tf_op jit(solution)/shard_map/ppermute | solution.py:16
  29.5 11.4 %copy-start = (bf16[3,3,32,48]{3,2,1,0:T(8,128)(2,1)S(1)}, bf16[3,3,32,48]{3,2,1,0:T(8,128)(2,1)}, u32[]{:S(2)}) copy-start(bf16[3,3,32,48]{3,2,1,0:T(8,128)(2,1)} %param.5) | copy-start | bytes 82948
  64.3 2.8 %copy-start.1 = (f32[32]{0:T(128)S(1)}, f32[32]{0:T(128)}, u32[]{:S(2)}) copy-start(f32[32]{0:T(128)} %param.6) | copy-start | bytes 388
  119.7 90.7 %all-to-all-start = ((bf16[32,8,4,128]{3,2,0,1:T(4,128)(2,1)}), bf16[32,8,4,128]{3,2,0,1:T(4,128)(2,1)S(1)}, u32[]{:S(2)}, u32[]{:S(2)}) async-start(bf16[32,8,4,128]{3,2,0,1:T(4,128)(2,1)} %copy.50), calls=%async_computation | async-start | bytes 524288 | tf_op jit(solution)/shard_map/all_to_all | solution.py:79
  126.3 75.1 %collective-permute-start.5 = (bf16[32,1,8,256]{3,0,2,1:T(8,128)(2,1)}, bf16[32,1,8,256]{3,0,2,1:T(8,128)(2,1)S(1)}, u32[]{:S(2)}, u32[]{:S(2)}) collective-permute-start(bf16[32,1,8,256]{3,0,2,1:T(8,128)(2,1)} %get-tuple-element.36), channel_id=1, source_target_pairs={{8,0},{16,8},{24,16},{32,24},{40,32},{48,40},{56,48},{64,56},{72,6... | collective-permute-start | bytes 393224 | tf_op jit(solution)/shard_map/ppermute | solution.py:19
  128.3 73.2 %collective-permute-start.4 = (bf16[32,1,8,256]{3,0,2,1:T(8,128)(2,1)}, bf16[32,1,8,256]{3,0,2,1:T(8,128)(2,1)S(1)}, u32[]{:S(2)}, u32[]{:S(2)}) collective-permute-start(bf16[32,1,8,256]{3,0,2,1:T(8,128)(2,1)} %get-tuple-element.35), channel_id=1, source_target_pairs={{0,8},{8,16},{16,24},{24,32},{32,40},{40,48},{48,56},{56,64},{64,7... | collective-permute-start | bytes 393224 | tf_op jit(solution)/shard_map/ppermute | solution.py:16
  202.4 11.3 %collective-permute-start.7 = (bf16[32,18,1,256]{3,0,2,1:T(8,128)(2,1)}, bf16[32,18,1,256]{3,0,2,1:T(8,128)(2,1)S(1)}, u32[]{:S(2)}, u32[]{:S(2)}) collective-permute-start(bf16[32,18,1,256]{3,0,2,1:T(8,128)(2,1)} %get-tuple-element.32), channel_id=1, source_target_pairs={{1,0},{2,1},{3,2},{4,3},{5,4},{6,5},{7,6},{9,8},{10,9},{11,10},{12... | collective-permute-start | bytes 884744 | tf_op jit(solution)/shard_map/ppermute | solution.py:19
  203.7 16.1 %collective-permute-start.6 = (bf16[32,18,1,256]{3,0,2,1:T(8,128)(2,1)}, bf16[32,18,1,256]{3,0,2,1:T(8,128)(2,1)S(1)}, u32[]{:S(2)}, u32[]{:S(2)}) collective-permute-start(bf16[32,18,1,256]{3,0,2,1:T(8,128)(2,1)} %get-tuple-element.31), channel_id=1, source_target_pairs={{0,1},{1,2},{2,3},{3,4},{4,5},{5,6},{6,7},{8,9},{9,10},{10,11},{11... | collective-permute-start | bytes 884744 | tf_op jit(solution)/shard_map/ppermute | solution.py:16
where the time goes:
time: 246 us; the launch traced here: 244 us
  blocking collectives  69.5 us (28%)
  matrix products  59 us (24%)
  local copies, waits for them, and re-layouts  43.4 us (18%)
  starting transfers between devices  32.9 us (13%)
  other arithmetic  28 us (11%)
  waiting for transfers between devices  10.4 us (4%)
    psum x1, blocking collectives, shards(): lax.psum((kernel_local, bias_local), ('depth', 'height'))  69.5 us
    dot_general x9, matrix products, shards(): jnp.einsum('ok,kdhw->odhw', kernel[row_tap, col_tap], window, preferred_e...  38 us
    ppermute x4, starting transfers between devices, with_halo(): lax.ppermute(lax.slice_in_dim(block, block.shape[dim] - width, None, axis...  19.9 us
    mul x2, local copies, waits for them, and re-layouts, shards(): upward = spread_cells(cotangent.astype(jnp.float32)) * 0.125  13.1 us
    reduce_sum x1, other arithmetic, pool_cells(): tensor.reshape(channels, depth_n // 2, 2, height_n // 2, 2, width_n // 2, 2)  13.1 us
    dot_general x9, matrix products, shards(): jnp.einsum('kc,kdhw->cdhw', back_kernel[row_tap, col_tap], window, prefer...  12.6 us
    add x1, local copies, waits for them, and re-layouts, smooth_leaky(): return leak_rate * values + (1.0 - leak_rate) * jax.nn.softplus(values)  10.4 us
    dot_general x9, matrix products, shards(): jnp.einsum('odhw,kdhw->ok', local_grad, source, preferred_element_type=jn...  8.47 us
  transfers between devices with their start and end apart: 9, of which 3 were waited for; matrix products, arithmetic and copies ran while one was open for 11% of the time, Pallas kernels for 0%

commit v1 on v0

v1 whole, which is shorter than its diff:
```python
import functools
import math

import jax
import jax.numpy as jnp
from jax import lax
from jax.experimental import pallas as pl
from jax.experimental.pallas import tpu as pltpu
from jax.sharding import PartitionSpec as P

BF = jnp.bfloat16
F32 = jnp.float32
MESH = pl.DeviceIdType.MESH

CI, CO, ND, NH, W = 16, 32, 16, 8, 256
ROWS = CO * NH
XROWS = CI * NH
KS = 512
ONES = 480
PAIRS = ND // 2


def dot(a, b):
    return jnp.dot(a, b, preferred_element_type=F32)


def dot_nt(a, b):
    return lax.dot_general(a, b, (((1,), (1,)), ((), ())), preferred_element_type=F32)


def iota(shape, dim):
    return lax.broadcasted_iota(jnp.int32, shape, dim)


def one_hot(cond, value=1.0):
    return jnp.where(cond, value, 0.0).astype(BF)


def shift_right(x):
    rolled = pltpu.roll(x, 1, 1)
    return jnp.where(iota(x.shape, 1) == 0, jnp.zeros_like(x), rolled)


def shift_left(x):
    rolled = pltpu.roll(x, x.shape[1] - 1, 1)
    return jnp.where(iota(x.shape, 1) == x.shape[1] - 1, jnp.zeros_like(x), rolled)


def kernel_body(nd, nh, vol, ker, bias, cot, pooled, gvol, gker, gbias,
                xa, ga, tm, tb, acc, om, um, hs, rh, rd, ps, rpool, ph, rp, rpc, pd, rpd, comp, rs, rs2, piece,
                full, s_v, r_v, s_p, r_p, s_g, r_g, s_a, r_a, s_b, r_b, s_c, r_c):
    i = lax.axis_index("depth")
    j = lax.axis_index("height")
    up_i, dn_i = lax.rem(i + 1, nd), lax.rem(i + nd - 1, nd)
    up_j, dn_j = lax.rem(j + 1, nh), lax.rem(j + nh - 1, nh)
    first_i, last_i = i == 0, i == nd - 1
    first_j, last_j = j == 0, j == nh - 1

    barrier = pltpu.get_barrier_semaphore()

    def greet_depth(k, carry):
        pl.semaphore_signal(barrier, inc=1, device_id=(lax.rem(i + k, nd), j), device_id_type=MESH)
        return carry

    def greet_height(k, carry):
        pl.semaphore_signal(barrier, inc=1, device_id=(i, lax.rem(j + k, nh)), device_id_type=MESH)
        return carry

    lax.fori_loop(1, nd, greet_depth, 0)
    lax.fori_loop(1, nh, greet_height, 0)
    for di in (dn_i, up_i):
        for dj in (dn_j, up_j):
            pl.semaphore_signal(barrier, inc=1, device_id=(di, dj), device_id_type=MESH)

    row, col = iota((2 * CI, XROWS), 0), iota((2 * CI, XROWS), 1)
    edge_rows = one_hot(col == (row % CI) * NH + (row // CI) * (NH - 1))
    for d in range(ND):
        x = vol[:, d].reshape(XROWS, W)
        edge = dot(edge_rows, x).astype(BF)
        hs[0, d] = edge[:CI]
        hs[1, d] = edge[CI:]

    pl.semaphore_wait(barrier, nd - 1 + nh - 1 + 4)

    def remote(src, dst, send, recv, target):
        return pltpu.make_async_remote_copy(
            src_ref=src, dst_ref=dst, send_sem=send, recv_sem=recv, device_id=target, device_id_type=MESH)

    vol_copies = [
        remote(hs.at[0], rh.at[1, pl.ds(1, ND)], s_v.at[0], r_v.at[0], (i, dn_j)),
        remote(hs.at[1], rh.at[0, pl.ds(1, ND)], s_v.at[1], r_v.at[1], (i, up_j)),
        remote(vol.at[:, 0], rd.at[1], s_v.at[2], r_v.at[2], (dn_i, j)),
        remote(vol.at[:, ND - 1], rd.at[0], s_v.at[3], r_v.at[3], (up_i, j)),
        remote(hs.at[0, 0], rh.at[1, ND + 1], s_v.at[4], r_v.at[4], (dn_i, dn_j)),
        remote(hs.at[0, ND - 1], rh.at[1, 0], s_v.at[5], r_v.at[5], (up_i, dn_j)),
        remote(hs.at[1, 0], rh.at[0, ND + 1], s_v.at[6], r_v.at[6], (dn_i, up_j)),
        remote(hs.at[1, ND - 1], rh.at[0, 0], s_v.at[7], r_v.at[7], (up_i, up_j)),
    ]
    for copy in vol_copies:
        copy.start()

    def put_slab(p, x):
        xa[p, 0:XROWS] = shift_right(x)
        xa[p, XROWS:2 * XROWS] = x
        xa[p, 2 * XROWS:3 * XROWS] = shift_left(x)

    for d in range(ND):
        put_slab(d + 1, vol[:, d].reshape(XROWS, W))

    row, col = iota((3 * CI, 640), 0), iota((3 * CI, 640), 1)
    expand = one_hot(((col < 384) & (row == col // NH))
                     | ((col >= 384) & (col < 512) & (row == col - 384))
                     | ((col >= 512) & (row + 3 * CI == col - 512)))
    lane_h = iota((CO, 384), 1) % NH
    for a in range(3):
        taps = dot(ker[a], expand)
        for h in range(NH):
            band = jnp.zeros((CO, 384), F32)
            for b in range(3):
                if 0 <= h + b - 1 < NH:
                    band = jnp.where(lane_h == h + b - 1, taps[b * CO:(b + 1) * CO, :384], band)
            tm[h * CO:(h + 1) * CO, a * KS:a * KS + 384] = band.astype(BF)
            if h == 0:
                side = taps[0:CO, 384:512].astype(BF)
            elif h == NH - 1:
                side = taps[2 * CO:3 * CO, 512:640].astype(BF)
            else:
                side = jnp.zeros((CO, 128), BF)
            tm[h * CO:(h + 1) * CO, a * KS + 384:(a + 1) * KS] = side
    for a in range(3):
        flipped = tm[:, a * KS:(a + 1) * KS].T
        for e in range(3):
            at = (2 - a) * 3 * ROWS + e * ROWS
            tb[0:XROWS, at:at + ROWS] = flipped[e * XROWS:(e + 1) * XROWS]
            tb[XROWS:XROWS + CI, at:at + ROWS] = flipped[384 + e * CI:384 + (e + 1) * CI]
            tb[XROWS + CI:XROWS + 2 * CI, at:at + ROWS] = flipped[432 + e * CI:432 + (e + 1) * CI]

    row, col = iota((128, 128), 0), iota((128, 128), 1)
    to_h_major = one_hot(col == (row % CO) * 4 + row // CO)
    to_o_major = one_hot(col == (row % 4) * CO + row // 4)
    spread = one_hot(iota((128, W), 0) == iota((128, W), 1) // 2)
    gather = one_hot((iota((2 * W, 128), 0) % W) // 2 == iota((2 * W, 128), 1), 0.125)
    for q in range(PAIRS):
        ct = cot[:, q].reshape(128, 128)
        um[q] = dot(dot(to_h_major, ct).astype(BF), spread)
    eye = iota((CO, CO), 0) == iota((CO, CO), 1)
    bias_col = jnp.sum(jnp.where(eye, jnp.broadcast_to(bias[...], (CO, CO)), 0.0), axis=1, keepdims=True)
    bias_rows = jnp.concatenate([bias_col] * NH, axis=0)

    ones_rows = one_hot(iota((KS - ONES, W), 0) == 0)
    for p in range(ND + 2):
        xa[p, ONES:KS] = ones_rows

    for copy in vol_copies:
        copy.wait_recv()
    zero_slab = jnp.zeros((XROWS, W), BF)
    put_slab(0, jnp.where(first_i, zero_slab, rd[0].reshape(XROWS, W)))
    put_slab(ND + 1, jnp.where(last_i, zero_slab, rd[1].reshape(XROWS, W)))
    for side in range(2):
        for p in range(ND + 2):
            outside = first_j if side == 0 else last_j
            if p == 0:
                outside = outside | first_i
            if p == ND + 1:
                outside = outside | last_i
            x = jnp.where(outside, jnp.zeros((CI, W), BF), rh[side, p])
            at = 384 + side * 48
            xa[p, at:at + CI] = shift_right(x)
            xa[p, at + CI:at + 2 * CI] = x
            xa[p, at + 2 * CI:at + 3 * CI] = shift_left(x)

    def forward(q, carry):
        cells = None
        for k in range(2):
            d = 2 * q + k
            before = dot(tm[...], xa[pl.ds(d, 3)].reshape(3 * KS, W)) + bias_rows
            th = jnp.tanh(0.5 * before)
            act = jnp.maximum(before, 0.3 * before) - 0.7 * jnp.log(0.5 + 0.5 * jnp.abs(th))
            slope = (0.08125 + 0.04375 * th).reshape(4, 2, CO, W)
            g = (um[q].reshape(4, 1, CO, W) * slope).reshape(ROWS, W).astype(BF)
            ga[d, 0:ROWS] = shift_left(g)
            ga[d, ROWS:2 * ROWS] = g
            ga[d, 2 * ROWS:3 * ROWS] = shift_right(g)
            part = act.reshape(4, 2, CO, W).sum(axis=1).reshape(128, W)
            cells = part if cells is None else cells + part
        high = cells.astype(BF)
        low = (cells - high.astype(F32)).astype(BF)
        mean = dot(jnp.concatenate([high, low], axis=1), gather).astype(BF)
        ps[q] = dot(to_o_major, mean).astype(BF).reshape(CO, 4, 128)
        return carry

    lax.fori_loop(0, PAIRS, forward, 0)

    def pool_copy(k):
        t = lax.rem(j + k, nh)
        return remote(ps.at[t], rpool.at[j], s_p.at[k], r_p.at[k], (i, t))

    def pool_start(k, carry):
        pool_copy(k).start()
        return carry

    lax.fori_loop(1, nh, pool_start, 0)
    rpool[j] = ps[j]

    acc[...] = jnp.zeros_like(acc)

    def taps_grad(q, carry):
        d = 4 * q
        left = jnp.concatenate([xa[pl.ds(d + k, 3)].reshape(3 * KS, W) for k in range(4)], axis=1)
        right = jnp.concatenate([ga[d + k, ROWS:2 * ROWS] for k in range(4)], axis=1)
        acc[...] += dot_nt(left, right)
        return carry

    lax.fori_loop(0, ND // 4, taps_grad, 0)

    sub, lane_at = iota((1, NH, W), 1), iota((1, NH, W), 2) // CO
    half_at = iota((48, W), 1) // CO
    lane_block = iota((48, 128), 1) // CO

    def fold(x):
        x = x[:, :128] + x[:, 128:]
        x = x + pltpu.roll(x, 64, 1)
        return x + pltpu.roll(x, 32, 1)

    comp[...] = jnp.zeros_like(comp)
    for a in range(3):
        own = acc[a * KS:a * KS + 384].reshape(48, NH, W)
        for b in range(3):
            t = a * 3 + b
            diag = jnp.sum(jnp.where(sub == lane_at + (b - 1), own, 0.0), axis=1)
            if b == 0:
                diag = diag + jnp.where(half_at == 0, acc[a * KS + 384:a * KS + 432], 0.0)
            if b == 2:
                diag = diag + jnp.where(half_at == NH - 1, acc[a * KS + 432:a * KS + 480], 0.0)
            diag = fold(diag)
            if t < 8:
                at = (t % 2) * 48
                comp[at:at + 48] += jnp.where(lane_block == t // 2, diag, 0.0)
            else:
                comp[96:128] += jnp.where(lane_block[:32] == 0, diag[:32], 0.0)
                comp[96:112] += jnp.where(lane_block[:16] == 1, diag[32:48], 0.0)
    comp[96:104] += jnp.where(lane_block[:8] == 2, fold(acc[KS + ONES:KS + ONES + 8]), 0.0)

    rows = 128 // nd

    def scatter_copy(k):
        t = lax.rem(i + k, nd)
        return remote(comp.at[pl.ds(pl.multiple_of(t * rows, rows), rows)], rs.at[i], s_a.at[k], r_a.at[k], (t, j))

    def all_copy(k):
        t = lax.rem(j + k, nh)
        return remote(piece, rs2.at[j], s_b.at[k], r_b.at[k], (i, t))

    def gather_copy(k):
        t = lax.rem(i + k, nd)
        here = full.at[pl.ds(pl.multiple_of(i * rows, rows), rows)]
        return remote(here, here, s_c.at[k], r_c.at[k], (t, j))

    def run(count, make, act):
        def step(k, carry):
            getattr(make(k), act)()
            return carry
        lax.fori_loop(1, count, step, 0)

    run(nd, scatter_copy, "start")
    rs[i] = comp[pl.ds(pl.multiple_of(i * rows, rows), rows)]

    def back(lo, hi, d):
        k0 = (lo - d + 1) * 3 * ROWS
        n = hi - lo
        return dot(tb[:, k0:k0 + n * 3 * ROWS], ga[lo:hi].reshape(n * 3 * ROWS, W))

    def keep(d, out):
        ph[0, d + 1] = out[XROWS:XROWS + CI].astype(BF)
        ph[1, d + 1] = out[XROWS + CI:].astype(BF)

    for side, d in ((0, -1), (1, ND)):
        out = back(max(d - 1, 0), min(d + 2, ND), d)
        pd[side] = out[:XROWS].astype(BF)
        keep(d, out)
    grad_copies = [
        remote(pd.at[0], rpd.at[1], s_g.at[0], r_g.at[0], (dn_i, j)),
        remote(pd.at[1], rpd.at[0], s_g.at[1], r_g.at[1], (up_i, j)),
        remote(ph.at[0, 0], rpc.at[1, 1], s_g.at[2], r_g.at[2], (dn_i, dn_j)),
        remote(ph.at[1, 0], rpc.at[1, 0], s_g.at[3], r_g.at[3], (dn_i, up_j)),
        remote(ph.at[0, ND + 1], rpc.at[0, 1], s_g.at[4], r_g.at[4], (up_i, dn_j)),
        remote(ph.at[1, ND + 1], rpc.at[0, 0], s_g.at[5], r_g.at[5], (up_i, up_j)),
    ]
    for copy in grad_copies:
        copy.start()

    def send_rows(n):
        part = pl.ds(1 + 4 * n, 4)
        for side, t in ((0, dn_j), (1, up_j)):
            at = 6 + 2 * n + side
            copy = remote(ph.at[side, part], rp.at[1 - side, pl.ds(4 * n, 4)], s_g.at[at], r_g.at[at], (i, t))
            copy.start()
            grad_copies.append(copy)

    for d in (0, ND - 1):
        out = back(max(d - 1, 0), min(d + 2, ND), d)
        om[d] = out[:XROWS]
        keep(d, out)

    def inner(d):
        out = dot(tb[...], ga[pl.ds(d - 1, 3)].reshape(9 * ROWS, W))
        om[d] = out[:XROWS]
        ph[0, d + 1] = out[XROWS:XROWS + CI].astype(BF)
        ph[1, d + 1] = out[XROWS + CI:].astype(BF)

    for d in (1, 2, 3):
        inner(d)
    send_rows(0)
    for d in (4, 5, 6, 7):
        inner(d)
    send_rows(1)

    run(nd, scatter_copy, "wait_recv")
    total = rs[0]
    for k in range(1, nd):
        total = total + rs[k]
    piece[...] = total
    rs2[j] = total
    run(nh, all_copy, "start")

    for d in (8, 9, 10, 11):
        inner(d)
    send_rows(2)
    for d in (12, 13, 14):
        inner(d)
    send_rows(3)

    run(nh, all_copy, "wait_recv")
    total = rs2[0]
    for k in range(1, nh):
        total = total + rs2[k]
    full[pl.ds(pl.multiple_of(i * rows, rows), rows)] = total
    run(nd, gather_copy, "start")

    run(nh, pool_copy, "wait_recv")
    for o in range(CO):
        pooled[o, 0] = rpool[:, o].reshape(4 * nh, 128)

    for copy in grad_copies:
        copy.wait_recv()
    row, col = iota((XROWS, 2 * CI), 0), iota((XROWS, 2 * CI), 1)
    place = one_hot(row == (col % CI) * NH + (col // CI) * (NH - 1))
    zero_rows = jnp.zeros((CI, W), BF)

    def edges(low, high, none):
        return dot(place, jnp.concatenate([jnp.where(first_j | none, zero_rows, low),
                                           jnp.where(last_j | none, zero_rows, high)], axis=0))

    for d in range(ND):
        out = om[d] + edges(rp[0, d], rp[1, d], False)
        if d in (0, ND - 1):
            side = 0 if d == 0 else 1
            none = first_i if d == 0 else last_i
            out = out + edges(rpc[side, 0], rpc[side, 1], none)
            out = out + jnp.where(none, zero_slab, rpd[side]).astype(F32)
        gvol[:, d] = out.astype(BF).reshape(CI, NH, W)

    run(nd, gather_copy, "wait_recv")
    norm = 1.0 / math.sqrt(float(ND * NH * W * nd * nh))
    final = full[...] * norm
    turned = final.T
    for t in range(8):
        gker[t // 3, t % 3] = turned[(t // 2) * CO:(t // 2 + 1) * CO, (t % 2) * 48:(t % 2 + 1) * 48]
    gker[2, 2, :, 0:32] = turned[0:CO, 96:128]
    gker[2, 2, :, 32:48] = turned[CO:2 * CO, 96:112]
    gbias[...] = final[96:97, 2 * CO:3 * CO]

    for copy in vol_copies + grad_copies:
        copy.wait_send()
    run(nh, pool_copy, "wait_send")
    run(nd, scatter_copy, "wait_send")
    run(nh, all_copy, "wait_send")
    run(nd, gather_copy, "wait_send")


def shards(nd, nh, volume, kernel, conv_bias, cotangent):
    vmem = pl.BlockSpec(memory_space=pltpu.VMEM)
    rows = 128 // nd
    dma = pltpu.SemaphoreType.DMA
    pooled, gvol, gker, gbias = pl.pallas_call(
        functools.partial(kernel_body, nd, nh),
        out_shape=(
            jax.ShapeDtypeStruct((CO, 1, 4 * nh, 128), BF),
            jax.ShapeDtypeStruct((CI, ND, NH, W), BF),
            jax.ShapeDtypeStruct((3, 3, CO, 3 * CI), F32),
            jax.ShapeDtypeStruct((1, CO), F32),
        ),
        in_specs=[vmem] * 4,
        out_specs=(vmem,) * 4,
        scratch_shapes=[
            pltpu.VMEM((ND + 2, KS, W), BF),
            pltpu.VMEM((ND, 3 * ROWS, W), BF),
            pltpu.VMEM((ROWS, 3 * KS), BF),
            pltpu.VMEM((XROWS + 2 * CI, 9 * ROWS), BF),
            pltpu.VMEM((3 * KS, ROWS), F32),
            pltpu.VMEM((ND, XROWS, W), F32),
            pltpu.VMEM((PAIRS, 128, W), F32),
            pltpu.VMEM((2, ND, CI, W), BF),
            pltpu.VMEM((2, ND + 2, CI, W), BF),
            pltpu.VMEM((2, CI, NH, W), BF),
            pltpu.VMEM((PAIRS, CO, 4, 128), BF),
            pltpu.VMEM((PAIRS, CO, 4, 128), BF),
            pltpu.VMEM((2, ND + 2, CI, W), BF),
            pltpu.VMEM((2, ND, CI, W), BF),
            pltpu.VMEM((2, 2, CI, W), BF),
            pltpu.VMEM((2, XROWS, W), BF),
            pltpu.VMEM((2, XROWS, W), BF),
            pltpu.VMEM((128, 128), F32),
            pltpu.VMEM((nd, rows, 128), F32),
            pltpu.VMEM((nh, rows, 128), F32),
            pltpu.VMEM((rows, 128), F32),
            pltpu.VMEM((128, 128), F32),
            dma((8,)), dma((8,)),
            dma((nh,)), dma((nh,)),
            dma((14,)), dma((14,)),
            dma((nd,)), dma((nd,)),
            dma((nh,)), dma((nh,)),
            dma((nd,)), dma((nd,)),
        ],
        compiler_params=pltpu.CompilerParams(
            collective_id=0, has_side_effects=True, vmem_limit_bytes=56 * 2**20),
        cost_estimate=pl.CostEstimate(flops=10 * 10**9, bytes_accessed=3 * 2**20, transcendentals=2 * 2**20),
        name="conv_step",
    )(volume, kernel.reshape(3, 3 * CO, 3 * CI), conv_bias.reshape(1, CO), cotangent)
    return pooled, gvol, gker, gbias.reshape(CO)


def solution(mesh):
    nd, nh = mesh.shape["depth"], mesh.shape["height"]
    in_specs = (P(None, "depth", "height", None), P(), P(), P(None, "depth", "height", None))
    out_specs = (
        P(None, ("depth", "height"), None, None),
        P(None, "depth", "height", None),
        P(),
        P(),
    )
    return jax.shard_map(
        functools.partial(shards, nd, nh), mesh=mesh, in_specs=in_specs, out_specs=out_specs, check_vma=False)
```

time: 246 us -> 56.9 us (0.23)
  blocking collectives: 69.5 us -> 0 us
  matrix products: 59 us -> 0 us
  Pallas kernels: 0 us -> 50.9 us
  local copies, waits for them, and re-layouts: 43.4 us -> 5.17 us
  starting transfers between devices: 32.9 us -> 0 us
  other arithmetic: 28 us -> 0 us
  waiting for transfers between devices: 10.4 us -> 0 us
    psum x1 -> x0, blocking collectives: 69.5 us -> none  [shards(): lax.psum((kernel_local, bias_local), ('depth', 'height'))]
    dot_general x27 -> x0, matrix products: 59 us -> none  [the longest x9 38 us: shards(): jnp.einsum('ok,kdhw->odhw', kernel[row_tap, col_tap], window, preferred_e...]
    pallas_call x0 -> x1, Pallas kernels: none -> 50.9 us  [shards(): pl.pallas_call(functools.partial(kernel_body, nd, nh), out_shape=(jax.Sha...]
    ppermute x8 -> x0, starting transfers between devices: 26.3 us -> none  [the longest x4 19.9 us: with_halo(): lax.ppermute(lax.slice_in_dim(block, block.shape[dim] - width, None, axis...]
    mul x2 -> x0, local copies, waits for them, and re-layouts: 13.1 us -> none  [shards(): upward = spread_cells(cotangent.astype(jnp.float32)) * 0.125]
    reduce_sum x1 -> x0, other arithmetic: 13.1 us -> none  [pool_cells(): tensor.reshape(channels, depth_n // 2, 2, height_n // 2, 2, width_n // 2, 2)]
    concatenate x4 -> x0, other arithmetic: 11 us -> none  [the longest x2 6.61 us: with_halo(): block = jnp.concatenate([low, block, high], axis=dim)]
    add x1 -> x0, local copies, waits for them, and re-layouts: 10.4 us -> none  [smooth_leaky(): return leak_rate * values + (1.0 - leak_rate) * jax.nn.softplus(values)]
  transfers between devices with their start and end apart: 9 -> 0, of which waited for: 3 -> 0; matrix products, arithmetic and copies ran while one was open for 11% -> 0% of each run, Pallas kernels for 0% -> 0%
where the time goes in v1:
time: 56.9 us; the launch traced here: 56.7 us
  Pallas kernels  50.9 us (89%)
  local copies, waits for them, and re-layouts  5.17 us (9%)
  between operations  0.64 us (1%)
    pallas_call x1, Pallas kernels, shards(): pl.pallas_call(functools.partial(kernel_body, nd, nh), out_shape=(jax.Sha...  50.9 us
    unnamed x8, local copies, waits for them, and re-layouts  5.17 us

profile of v1, /device:TPU:1, one launch (start us, length us, event | category | flops | bytes accessed | tf_op | source)
XLA Modules:
  0.0 56.7 jit_solution(10835186086407669652)
XLA Ops:
  0.6 50.9 %conv_step.1 = (bf16[32,1,32,128]{3,2,1,0:T(8,128)(2,1)}, bf16[16,16,8,256]{3,2,1,0:T(8,128)(2,1)}, f32[3,3,32,48]{3,2,1,0:T(8,128)}, f32[1,32]{1,0:T(1,128)}) custom-call(bf16[16,16,8,256]{3,2,1,0:T(8,128)(2,1)} %vol.1, bf16[3,96,48]{2,1,0:T(8,128)(2,1)} %bitcast.3, f32[1,32]{1,0:T(1,128)} %bitcast.4, bf16[32,8,4,128]{3,2,1,0:T(4,128)(2,1)} %cot.1), custom_call_target="tpu_custom_call" | custom-call | flops 10000000000 | bytes 3145728 | tf_op jit(solution)/shard_map/conv_step/pallas_call | solution.py:385
  51.6 1.7 %copy.12 = bf16[32,1,32,128]{3,2,1,0:T(8,128)(2,1)} copy(bf16[32,1,32,128]{3,2,1,0:T(8,128)(2,1)} %get-tuple-element.16) | data formatting | bytes 524288
  53.2 0.0 copy-start
  53.2 2.3 %copy.13 = bf16[16,16,8,256]{3,2,1,0:T(8,128)(2,1)} copy(bf16[16,16,8,256]{3,2,1,0:T(8,128)(2,1)} %get-tuple-element.17) | data formatting | bytes 2097152
  55.6 0.0 copy-done
  55.6 0.0 copy-start.1
  55.6 0.7 %copy.14 = f32[3,3,32,48]{3,2,1,0:T(8,128)} copy(f32[3,3,32,48]{3,2,1,0:T(8,128)S(1)} %copy-done) | data formatting | bytes 110592
  56.2 0.0 copy-done.1
  56.2 0.5 copy.15
Async XLA Ops:
  53.2 2.3 %copy-start = (f32[3,3,32,48]{3,2,1,0:T(8,128)S(1)}, f32[3,3,32,48]{3,2,1,0:T(8,128)}, u32[]{:S(2)}) copy-start(f32[3,3,32,48]{3,2,1,0:T(8,128)} %get-tuple-element.18) | copy-start | bytes 165892
  55.6 0.7 %copy-start.1 = (f32[1,32]{1,0:T(1,128)S(1)}, f32[1,32]{1,0:T(1,128)}, u32[]{:S(2)}) copy-start(f32[1,32]{1,0:T(1,128)} %get-tuple-element.11) | copy-start | bytes 388

commit v2 on v1

v2 whole, which is shorter than its diff:
```python
import functools
import math

import jax
import jax.numpy as jnp
from jax import lax
from jax.experimental import pallas as pl
from jax.experimental.pallas import tpu as pltpu
from jax.sharding import PartitionSpec as P

BF = jnp.bfloat16
F32 = jnp.float32
MESH = pl.DeviceIdType.MESH

CI, CO, ND, NH, W = 16, 32, 16, 8, 256
ROWS = CO * NH
XROWS = CI * NH
KM = 3 * XROWS
ONES = 96
PAIRS = ND // 2
RING = 4
NEAR = 8
FAR = RING * RING
PIECE = 128 // NEAR


def dot(a, b):
    return jnp.dot(a, b, preferred_element_type=F32)


def dot_nt(a, b):
    return lax.dot_general(a, b, (((1,), (1,)), ((), ())), preferred_element_type=F32)


def iota(shape, dim):
    return lax.broadcasted_iota(jnp.int32, shape, dim)


def one_hot(cond, value=1.0):
    return jnp.where(cond, value, 0.0).astype(BF)


def shift_right(x):
    rolled = pltpu.roll(x, 1, 1)
    return jnp.where(iota(x.shape, 1) == 0, jnp.zeros_like(x), rolled)


def shift_left(x):
    rolled = pltpu.roll(x, x.shape[1] - 1, 1)
    return jnp.where(iota(x.shape, 1) == x.shape[1] - 1, jnp.zeros_like(x), rolled)


def kernel_body(nd, nh, vol_in, ker, bias, cot_in, pooled, gvol, gker, gbias,
                vol, cot, xa, xh, ga, tm, th, tb, acc, bm, om, um, cells, hs, rh, rd, ps, rpool, ph, rp, rpc, pd, rpd, comp, rs, rs2, piece,
                full, s_in, s_v, r_v, s_p, r_p, s_g, r_g, s_a, r_a, s_b, r_b, s_c, r_c):
    i = lax.axis_index("depth")
    j = lax.axis_index("height")
    up_i, dn_i = lax.rem(i + 1, nd), lax.rem(i + nd - 1, nd)
    up_j, dn_j = lax.rem(j + 1, nh), lax.rem(j + nh - 1, nh)
    first_i, last_i = i == 0, i == nd - 1
    first_j, last_j = j == 0, j == nh - 1
    near = lax.rem(j, 2) * 4 + lax.rem(i, 4)
    far = (i // 4) * RING + j // 2

    def near_target(k):
        t = lax.rem(near + k, NEAR)
        return t, ((i // 4) * 4 + lax.rem(t, 4), (j // 2) * 2 + t // 4)

    def far_target(k):
        t = lax.rem(far + k, FAR)
        return t, ((t // RING) * 4 + lax.rem(i, 4), lax.rem(t, RING) * 2 + lax.rem(j, 2))

    def high_target(k):
        t = lax.rem(j + k, nh)
        return t, (i, t)

    vol_load = pltpu.make_async_copy(vol_in, vol, s_in.at[0])
    cot_load = pltpu.make_async_copy(cot_in, cot, s_in.at[1])
    vol_load.start()
    cot_load.start()
    barrier = pltpu.get_barrier_semaphore()

    def greet(target):
        pl.semaphore_signal(barrier, inc=1, device_id=target, device_id_type=MESH)

    def greet_all(count, make):
        def step(k, carry):
            greet(make(k)[1])
            return carry
        lax.fori_loop(1, count, step, 0)

    for di in (dn_i, up_i):
        for dj in (dn_j, j, up_j):
            greet((di, dj))
    greet_all(nh, high_target)
    greet_all(NEAR, near_target)
    greet_all(FAR, far_target)

    row, col = iota((2 * CI, XROWS), 0), iota((2 * CI, XROWS), 1)
    edge_rows = one_hot(col == (row % CI) * NH + (row // CI) * (NH - 1))
    vol_load.wait()
    for d in range(ND):
        edge = dot(edge_rows, vol[:, d].reshape(XROWS, W)).astype(BF)
        hs[0, d] = edge[:CI]
        hs[1, d] = edge[CI:]

    pl.semaphore_wait(barrier, 6 + nh - 1 + NEAR - 1 + FAR - 1)

    def remote(src, dst, send, recv, target):
        return pltpu.make_async_remote_copy(
            src_ref=src, dst_ref=dst, send_sem=send, recv_sem=recv, device_id=target, device_id_type=MESH)

    vol_copies = [
        remote(vol.at[:, 0], rd.at[1], s_v.at[0], r_v.at[0], (dn_i, j)),
        remote(vol.at[:, ND - 1], rd.at[0], s_v.at[1], r_v.at[1], (up_i, j)),
        remote(hs.at[0, 0], rh.at[1, ND + 1], s_v.at[2], r_v.at[2], (dn_i, dn_j)),
        remote(hs.at[0, ND - 1], rh.at[1, 0], s_v.at[3], r_v.at[3], (up_i, dn_j)),
        remote(hs.at[1, 0], rh.at[0, ND + 1], s_v.at[4], r_v.at[4], (dn_i, up_j)),
        remote(hs.at[1, ND - 1], rh.at[0, 0], s_v.at[5], r_v.at[5], (up_i, up_j)),
        remote(hs.at[0], rh.at[1, pl.ds(1, ND)], s_v.at[6], r_v.at[6], (i, dn_j)),
        remote(hs.at[1], rh.at[0, pl.ds(1, ND)], s_v.at[7], r_v.at[7], (i, up_j)),
    ]
    for copy in vol_copies:
        copy.start()

    def put_slab(p, x):
        xa[p, 0:XROWS] = shift_right(x)
        xa[p, XROWS:2 * XROWS] = x
        xa[p, 2 * XROWS:3 * XROWS] = shift_left(x)

    for d in range(ND):
        put_slab(d + 1, vol[:, d].reshape(XROWS, W))

    row, col = iota((3 * CI, 640), 0), iota((3 * CI, 640), 1)
    expand = one_hot(((col < 384) & (row == col // NH))
                     | ((col >= 384) & (col < 512) & (row == col - 384))
                     | ((col >= 512) & (row + 3 * CI == col - 512)))
    lane_h = iota((CO, 384), 1) % NH
    for a in range(3):
        taps = dot(ker[a], expand)
        for h in range(NH):
            band = jnp.zeros((CO, 384), F32)
            for b in range(3):
                if 0 <= h + b - 1 < NH:
                    band = jnp.where(lane_h == h + b - 1, taps[b * CO:(b + 1) * CO, :384], band)
            tm[h * CO:(h + 1) * CO, a * KM:(a + 1) * KM] = band.astype(BF)
        th[0:CO, a * 128:(a + 1) * 128] = taps[0:CO, 384:512].astype(BF)
        th[CO:2 * CO, a * 128:(a + 1) * 128] = taps[2 * CO:3 * CO, 512:640].astype(BF)

    def own_part(d):
        lo, hi = max(d, 1), min(d + 3, ND + 1)
        k0 = (lo - d) * KM
        bm[d] = dot(tm[:, k0:k0 + (hi - lo) * KM], xa[lo:hi].reshape((hi - lo) * KM, W))

    def own_parts(n, carry):
        for k in range(7):
            d = 1 + 7 * n + k
            bm[d] = dot(tm[...], xa[pl.ds(d, 3)].reshape(3 * KM, W))
        return carry

    lax.fori_loop(0, 2, own_parts, 0)
    own_part(0)
    own_part(ND - 1)

    row, col = iota((128, 128), 0), iota((128, 128), 1)
    to_h_major = one_hot(col == (row % CO) * 4 + row // CO)
    to_o_major = one_hot(col == (row % 4) * CO + row // 4)
    spread = one_hot(iota((128, W), 0) == iota((128, W), 1) // 2)
    gather = one_hot((iota((2 * W, 128), 0) % W) // 2 == iota((2 * W, 128), 1), 0.125)
    cot_load.wait()
    for q in range(PAIRS):
        ct = cot[:, q].reshape(128, 128)
        um[q] = dot(dot(to_h_major, ct).astype(BF), spread)
    eye = iota((CO, CO), 0) == iota((CO, CO), 1)
    bias_col = jnp.sum(jnp.where(eye, jnp.broadcast_to(bias[...], (CO, CO)), 0.0), axis=1, keepdims=True)
    bias_rows = jnp.concatenate([bias_col] * NH, axis=0)

    ones_rows = one_hot(iota((128 - ONES, W), 0) == 0)
    for p in range(ND + 2):
        xh[p, ONES:128] = ones_rows

    for a in range(3):
        flipped = tm[:, a * KM:(a + 1) * KM].T
        side = jnp.concatenate([th[0:CO, a * 128:(a + 1) * 128], jnp.zeros((ROWS - 2 * CO, 128), BF),
                                th[CO:2 * CO, a * 128:(a + 1) * 128]], axis=0).T
        for e in range(3):
            at = (2 - a) * 3 * ROWS + e * ROWS
            tb[0:XROWS, at:at + ROWS] = flipped[e * XROWS:(e + 1) * XROWS]
            tb[XROWS:XROWS + CI, at:at + ROWS] = side[e * CI:(e + 1) * CI]
            tb[XROWS + CI:XROWS + 2 * CI, at:at + ROWS] = side[48 + e * CI:48 + (e + 1) * CI]

    for copy in vol_copies:
        copy.wait_recv()
    zero_slab = jnp.zeros((XROWS, W), BF)
    put_slab(0, jnp.where(first_i, zero_slab, rd[0].reshape(XROWS, W)))
    put_slab(ND + 1, jnp.where(last_i, zero_slab, rd[1].reshape(XROWS, W)))
    for p in range(ND + 2):
        edge = first_i if p == 0 else last_i if p == ND + 1 else False
        for side, outside in ((0, first_j), (1, last_j)):
            x = jnp.where(outside | edge, jnp.zeros((CI, W), BF), rh[side, p])
            at = side * 48
            xh[p, at:at + CI] = shift_right(x)
            xh[p, at + CI:at + 2 * CI] = x
            xh[p, at + 2 * CI:at + 3 * CI] = shift_left(x)
    bm[0] += dot(tm[:, 0:KM], xa[0])
    bm[ND - 1] += dot(tm[:, 2 * KM:3 * KM], xa[ND + 1])

    def forward(q):
        total = None
        for k in range(2):
            d = 2 * q + k
            rim = dot(th[...], xh[pl.ds(d, 3)].reshape(3 * 128, W))
            own = bm[d]
            before = jnp.concatenate([own[:CO] + rim[:CO], own[CO:ROWS - CO], own[ROWS - CO:] + rim[CO:]], axis=0)
            before = before + bias_rows
            t = jnp.tanh(0.5 * before)
            act = jnp.maximum(before, 0.3 * before) - 0.7 * jnp.log(0.5 + 0.5 * jnp.abs(t))
            slope = (0.08125 + 0.04375 * t).reshape(4, 2, CO, W)
            ga[d, ROWS:2 * ROWS] = (um[q].reshape(4, 1, CO, W) * slope).reshape(ROWS, W).astype(BF)
            part = act.reshape(4, 2, CO, W).sum(axis=1).reshape(128, W)
            total = part if total is None else total + part
        cells[q] = total

    acc[...] = jnp.zeros_like(acc)

    def stage(s, carry):
        forward(2 * s)
        forward(2 * s + 1)
        ds = [4 * s + k for k in range(4)]
        right = jnp.concatenate([ga[d, ROWS:2 * ROWS] for d in ds], axis=1)
        acc[0:3 * KM] += dot_nt(jnp.concatenate([xa[pl.ds(d, 3)].reshape(3 * KM, W) for d in ds], axis=1), right)
        acc[3 * KM:] += dot_nt(jnp.concatenate([xh[pl.ds(d, 3)].reshape(3 * 128, W) for d in ds], axis=1), right)
        return carry

    lax.fori_loop(0, ND // 4, stage, 0)

    def run(count, make, act):
        def step(k, carry):
            getattr(make(k), act)()
            return carry
        lax.fori_loop(1, count, step, 0)

    def pool_copy(k):
        t, target = high_target(k)
        return remote(ps.at[t], rpool.at[j], s_p.at[k], r_p.at[k], target)

    sub, lane_at = iota((1, NH, W), 1), iota((1, NH, W), 2) // CO
    half_at = iota((48, W), 1) // CO
    lane_block = iota((48, 128), 1) // CO

    def fold(x):
        x = x[:, :128] + x[:, 128:]
        x = x + pltpu.roll(x, 64, 1)
        return x + pltpu.roll(x, 32, 1)

    comp[...] = jnp.zeros_like(comp)
    for a in range(3):
        own = acc[a * KM:(a + 1) * KM].reshape(48, NH, W)
        side = 3 * KM + a * 128
        for b in range(3):
            t = a * 3 + b
            diag = jnp.sum(jnp.where(sub == lane_at + (b - 1), own, 0.0), axis=1)
            if b == 0:
                diag = diag + jnp.where(half_at == 0, acc[side:side + 48], 0.0)
            if b == 2:
                diag = diag + jnp.where(half_at == NH - 1, acc[side + 48:side + 96], 0.0)
            diag = fold(diag)
            if t < 8:
                at = (t % 2) * 48
                comp[at:at + 48] += jnp.where(lane_block == t // 2, diag, 0.0)
            else:
                comp[96:128] += jnp.where(lane_block[:32] == 0, diag[:32], 0.0)
                comp[96:112] += jnp.where(lane_block[:16] == 1, diag[32:48], 0.0)
    comp[96:104] += jnp.where(lane_block[:8] == 2, fold(acc[3 * KM + 128 + ONES:3 * KM + 128 + ONES + 8]), 0.0)

    def scatter_copy(k):
        t, target = near_target(k)
        return remote(comp.at[pl.ds(pl.multiple_of(t * PIECE, PIECE), PIECE)], rs.at[near], s_a.at[k], r_a.at[k], target)

    def all_copy(k):
        return remote(piece, rs2.at[far], s_b.at[k], r_b.at[k], far_target(k)[1])

    own_piece = pl.ds(pl.multiple_of(near * PIECE, PIECE), PIECE)

    def gather_copy(k):
        here = full.at[own_piece]
        return remote(here, here, s_c.at[k], r_c.at[k], near_target(k)[1])

    run(NEAR, scatter_copy, "start")
    rs[near] = comp[own_piece]

    for q in range(PAIRS):
        total = cells[q]
        high = total.astype(BF)
        low = (total - high.astype(F32)).astype(BF)
        mean = dot(jnp.concatenate([high, low], axis=1), gather).astype(BF)
        ps[q] = dot(to_o_major, mean).astype(BF).reshape(CO, 4, 128)
    run(nh, pool_copy, "start")
    rpool[j] = ps[j]

    for d in range(ND):
        g = ga[d, ROWS:2 * ROWS]
        ga[d, 0:ROWS] = shift_left(g)
        ga[d, 2 * ROWS:3 * ROWS] = shift_right(g)

    def back(d):
        lo, hi = max(d - 1, 0), min(d + 2, ND)
        k0 = (lo - d + 1) * 3 * ROWS
        n = hi - lo
        return dot(tb[:, k0:k0 + n * 3 * ROWS], ga[lo:hi].reshape(n * 3 * ROWS, W))

    def keep(d, out):
        ph[0, d + 1] = out[XROWS:XROWS + CI].astype(BF)
        ph[1, d + 1] = out[XROWS + CI:].astype(BF)

    for side, d in ((0, -1), (1, ND)):
        out = back(d)
        pd[side] = out[:XROWS].astype(BF)
        keep(d, out)
    grad_copies = [
        remote(pd.at[0], rpd.at[1], s_g.at[0], r_g.at[0], (dn_i, j)),
        remote(pd.at[1], rpd.at[0], s_g.at[1], r_g.at[1], (up_i, j)),
        remote(ph.at[0, 0], rpc.at[1, 1], s_g.at[2], r_g.at[2], (dn_i, dn_j)),
        remote(ph.at[1, 0], rpc.at[1, 0], s_g.at[3], r_g.at[3], (dn_i, up_j)),
        remote(ph.at[0, ND + 1], rpc.at[0, 1], s_g.at[4], r_g.at[4], (up_i, dn_j)),
        remote(ph.at[1, ND + 1], rpc.at[0, 0], s_g.at[5], r_g.at[5], (up_i, up_j)),
    ]
    for copy in grad_copies:
        copy.start()

    def send_rows(n, d, count):
        for side, t in ((0, dn_j), (1, up_j)):
            at = 6 + 2 * n + side
            copy = remote(ph.at[side, pl.ds(d + 1, count)], rp.at[1 - side, pl.ds(d, count)],
                          s_g.at[at], r_g.at[at], (i, t))
            copy.start()
            grad_copies.append(copy)

    for d in (0, ND - 1):
        out = back(d)
        om[d] = out[:XROWS]
        keep(d, out)

    run(NEAR, scatter_copy, "wait_recv")
    total = rs[0]
    for k in range(1, NEAR):
        total = total + rs[k]
    piece[...] = total
    rs2[far] = total
    run(FAR, all_copy, "start")

    def inner(d0, count):
        def step(n, carry):
            for k in range(2):
                d = d0 + 2 * n + k
                out = dot(tb[...], ga[pl.ds(d - 1, 3)].reshape(9 * ROWS, W))
                om[d] = out[:XROWS]
                ph[0, d + 1] = out[XROWS:XROWS + CI].astype(BF)
                ph[1, d + 1] = out[XROWS + CI:].astype(BF)
            return carry
        lax.fori_loop(0, count // 2, step, 0)

    inner(1, 4)
    send_rows(0, 0, 5)
    inner(5, 4)
    send_rows(1, 5, 4)
    inner(9, 6)
    send_rows(2, 9, 7)

    run(FAR, all_copy, "wait_recv")
    total = rs2[0]
    for k in range(1, FAR):
        total = total + rs2[k]
    full[own_piece] = total
    run(NEAR, gather_copy, "start")

    run(nh, pool_copy, "wait_recv")
    for o in range(CO):
        pooled[o, 0] = rpool[:, o].reshape(4 * nh, 128)

    for copy in grad_copies:
        copy.wait_recv()
    row, col = iota((XROWS, 2 * CI), 0), iota((XROWS, 2 * CI), 1)
    place = one_hot(row == (col % CI) * NH + (col // CI) * (NH - 1))
    zero_rows = jnp.zeros((CI, W), BF)

    def edges(low, high, none):
        return dot(place, jnp.concatenate([jnp.where(first_j | none, zero_rows, low),
                                           jnp.where(last_j | none, zero_rows, high)], axis=0))

    for d in range(ND):
        out = om[d] + edges(rp[0, d], rp[1, d], False)
        if d in (0, ND - 1):
            side = 0 if d == 0 else 1
            none = first_i if d == 0 else last_i
            out = out + edges(rpc[side, 0], rpc[side, 1], none)
            out = out + jnp.where(none, zero_slab, rpd[side]).astype(F32)
        gvol[:, d] = out.astype(BF).reshape(CI, NH, W)

    run(NEAR, gather_copy, "wait_recv")
    norm = 1.0 / math.sqrt(float(ND * NH * W * nd * nh))
    final = full[...] * norm
    turned = final.T
    for t in range(8):
        gker[t // 3, t % 3] = turned[(t // 2) * CO:(t // 2 + 1) * CO, (t % 2) * 48:(t % 2 + 1) * 48]
    gker[2, 2, :, 0:32] = turned[0:CO, 96:128]
    gker[2, 2, :, 32:48] = turned[CO:2 * CO, 96:112]
    gbias[...] = final[96:97, 2 * CO:3 * CO]

    for copy in vol_copies + grad_copies:
        copy.wait_send()
    run(nh, pool_copy, "wait_send")
    run(NEAR, scatter_copy, "wait_send")
    run(FAR, all_copy, "wait_send")
    run(NEAR, gather_copy, "wait_send")


def hand_over(*refs):
    n = len(refs) // 2
    for k in range(n):
        refs[n + k][...] = refs[k][...]


def shards(nd, nh, volume, kernel, conv_bias, cotangent):
    vmem = pl.BlockSpec(memory_space=pltpu.VMEM)
    anywhere = pl.BlockSpec(memory_space=pl.ANY)
    dma = pltpu.SemaphoreType.DMA
    out_shape = (
        jax.ShapeDtypeStruct((CO, 1, 4 * nh, 128), BF),
        jax.ShapeDtypeStruct((CI, ND, NH, W), BF),
        jax.ShapeDtypeStruct((3, 3, CO, 3 * CI), F32),
        jax.ShapeDtypeStruct((1, CO), F32),
    )
    results = pl.pallas_call(
        functools.partial(kernel_body, nd, nh),
        out_shape=out_shape,
        in_specs=[anywhere, vmem, vmem, anywhere],
        out_specs=(vmem,) * 4,
        scratch_shapes=[
            pltpu.VMEM((CI, ND, NH, W), BF),
            pltpu.VMEM((CO, PAIRS, 4, 128), BF),
            pltpu.VMEM((ND + 2, KM, W), BF),
            pltpu.VMEM((ND + 2, 128, W), BF),
            pltpu.VMEM((ND, 3 * ROWS, W), BF),
            pltpu.VMEM((ROWS, 3 * KM), BF),
            pltpu.VMEM((2 * CO, 3 * 128), BF),
            pltpu.VMEM((XROWS + 2 * CI, 9 * ROWS), BF),
            pltpu.VMEM((3 * KM + 3 * 128, ROWS), F32),
            pltpu.VMEM((ND, ROWS, W), F32),
            pltpu.VMEM((ND, XROWS, W), F32),
            pltpu.VMEM((PAIRS, 128, W), F32),
            pltpu.VMEM((PAIRS, 128, W), F32),
            pltpu.VMEM((2, ND, CI, W), BF),
            pltpu.VMEM((2, ND + 2, CI, W), BF),
            pltpu.VMEM((2, CI, NH, W), BF),
            pltpu.VMEM((PAIRS, CO, 4, 128), BF),
            pltpu.VMEM((PAIRS, CO, 4, 128), BF),
            pltpu.VMEM((2, ND + 2, CI, W), BF),
            pltpu.VMEM((2, ND, CI, W), BF),
            pltpu.VMEM((2, 2, CI, W), BF),
            pltpu.VMEM((2, XROWS, W), BF),
            pltpu.VMEM((2, XROWS, W), BF),
            pltpu.VMEM((128, 128), F32),
            pltpu.VMEM((NEAR, PIECE, 128), F32),
            pltpu.VMEM((FAR, PIECE, 128), F32),
            pltpu.VMEM((PIECE, 128), F32),
            pltpu.VMEM((128, 128), F32),
            dma((2,)),
            dma((8,)), dma((8,)),
            dma((nh,)), dma((nh,)),
            dma((12,)), dma((12,)),
            dma((NEAR,)), dma((NEAR,)),
            dma((FAR,)), dma((FAR,)),
            dma((NEAR,)), dma((NEAR,)),
        ],
        compiler_params=pltpu.CompilerParams(
            collective_id=0, has_side_effects=True, vmem_limit_bytes=58 * 2**20),
        cost_estimate=pl.CostEstimate(flops=10 * 10**9, bytes_accessed=3 * 2**20, transcendentals=2 * 2**20),
        name="conv_step",
    )(volume, kernel.reshape(3, 3 * CO, 3 * CI), conv_bias.reshape(1, CO), cotangent)
    pooled, gvol, gker, gbias = pl.pallas_call(
        hand_over,
        out_shape=out_shape,
        in_specs=[vmem] * 4,
        out_specs=(vmem,) * 4,
        name="hand_over",
    )(*results)
    return pooled, gvol, gker, gbias.reshape(CO)


def solution(mesh):
    nd, nh = mesh.shape["depth"], mesh.shape["height"]
    in_specs = (P(None, "depth", "height", None), P(), P(), P(None, "depth", "height", None))
    out_specs = (
        P(None, ("depth", "height"), None, None),
        P(None, "depth", "height", None),
        P(),
        P(),
    )
    return jax.shard_map(
        functools.partial(shards, nd, nh), mesh=mesh, in_specs=in_specs, out_specs=out_specs, check_vma=False)
```

time: 56.9 us -> 47.7 us (0.84)
  local copies, waits for them, and re-layouts: 5.17 us -> 0 us
  Pallas kernels: 50.9 us -> 46.9 us
    unnamed x8 -> x0, local copies, waits for them, and re-layouts: 5.17 us -> none
    pallas_call x1 -> x2, Pallas kernels: 50.9 us -> 46.9 us  [the longest x1 44.4 us: shards(): pl.pallas_call(functools.partial(kernel_body, nd, nh), out_shape=out_shap...]
where the time goes in v2:
time: 47.7 us; the launch traced here: 47.5 us
  Pallas kernels  46.9 us (98%)
  between operations  0.64 us (1%)
    pallas_call x1, Pallas kernels, shards(): pl.pallas_call(functools.partial(kernel_body, nd, nh), out_shape=out_shap...  44.4 us
    pallas_call x1, Pallas kernels, shards(): pl.pallas_call(hand_over, out_shape=out_shape, in_specs=[vmem] * 4, out_s...  2.47 us

profile of v2, /device:TPU:1, one launch (start us, length us, event | category | flops | bytes accessed | tf_op | source)
XLA Modules:
  0.0 47.5 jit_solution(11768082843878253784)
XLA Ops:
  0.6 44.4 %conv_step.1 = (bf16[32,1,32,128]{3,2,1,0:T(8,128)(2,1)}, bf16[16,16,8,256]{3,2,1,0:T(8,128)(2,1)}, f32[3,3,32,48]{3,2,1,0:T(8,128)}, f32[1,32]{1,0:T(1,128)}) custom-call(bf16[16,16,8,256]{3,2,1,0:T(8,128)(2,1)} %vol_in.1, bf16[3,96,48]{2,1,0:T(8,128)(2,1)} %bitcast.3, f32[1,32]{1,0:T(1,128)} %bitcast.4, bf16[32,8,4,128]{3,2,1,0:T(4,128)(2,1)} %cot_in.1), custom_call_target="tpu_custom_call" | custom-call | flops 10000000000 | bytes 3145728 | tf_op jit(solution)/shard_map/conv_step/pallas_call | solution.py:434
  45.0 2.5 %hand_over.1 = (bf16[32,1,32,128]{3,2,1,0:T(8,128)(2,1)}, bf16[16,16,8,256]{3,2,1,0:T(8,128)(2,1)}, f32[3,3,32,48]{3,2,1,0:T(8,128)}, f32[1,32]{1,0:T(1,128)}) custom-call(bf16[32,1,32,128]{3,2,1,0:T(8,128)(2,1)} %get-tuple-element.12.refs_0_, bf16[16,16,8,256]{3,2,1,0:T(8,128)(2,1)} %get-tuple-element.13.refs_1_, ...), custom_call_target="tpu_custom_call" | custom-call | tf_op jit(solution)/shard_map/hand_over/pallas_call | solution.py:481

commit v3 on v2

--- a/solution.py
+++ b/solution.py
@@ -52,7 +52,7 @@
 
 def kernel_body(nd, nh, vol_in, ker, bias, cot_in, pooled, gvol, gker, gbias,
                 vol, cot, xa, xh, ga, tm, th, tb, acc, bm, om, um, cells, hs, rh, rd, ps, rpool, ph, rp, rpc, pd, rpd, comp, rs, rs2, piece,
-                full, s_in, s_v, r_v, s_p, r_p, s_g, r_g, s_a, r_a, s_b, r_b, s_c, r_c):
+                full, s_in, s_v, r_v, s_p, r_p, s_g, r_g, s_a, r_a, s_b, r_b, s_c, r_c, known):
     i = lax.axis_index("depth")
     j = lax.axis_index("height")
     up_i, dn_i = lax.rem(i + 1, nd), lax.rem(i + nd - 1, nd)
@@ -80,21 +80,16 @@
     cot_load.start()
     barrier = pltpu.get_barrier_semaphore()
 
-    def greet(target):
-        pl.semaphore_signal(barrier, inc=1, device_id=target, device_id_type=MESH)
-
-    def greet_all(count, make):
-        def step(k, carry):
-            greet(make(k)[1])
-            return carry
-        lax.fori_loop(1, count, step, 0)
-
-    for di in (dn_i, up_i):
-        for dj in (dn_j, j, up_j):
-            greet((di, dj))
-    greet_all(nh, high_target)
-    greet_all(NEAR, near_target)
-    greet_all(FAR, far_target)
+    def greet(sem, targets):
+        for target in targets:
+            pl.semaphore_signal(sem, inc=1, device_id=target, device_id_type=MESH)
+
+    def around(n):
+        at_i = (lax.rem(i + nd - n, nd), i, lax.rem(i + n, nd))
+        at_j = (lax.rem(j + nh - n, nh), j, lax.rem(j + n, nh))
+        return [(at_i[a], at_j[b]) for a in range(3) for b in range(3) if (a, b) != (1, 1)]
+
+    greet(barrier, around(1))
 
     row, col = iota((2 * CI, XROWS), 0), iota((2 * CI, XROWS), 1)
     edge_rows = one_hot(col == (row % CI) * NH + (row // CI) * (NH - 1))
@@ -104,7 +99,8 @@
         hs[0, d] = edge[:CI]
         hs[1, d] = edge[CI:]
 
-    pl.semaphore_wait(barrier, 6 + nh - 1 + NEAR - 1 + FAR - 1)
+    pl.semaphore_wait(barrier, 8)
+    greet(known.at[0], around(1))
 
     def remote(src, dst, send, recv, target):
         return pltpu.make_async_remote_copy(
@@ -147,6 +143,9 @@
         th[0:CO, a * 128:(a + 1) * 128] = taps[0:CO, 384:512].astype(BF)
         th[CO:2 * CO, a * 128:(a + 1) * 128] = taps[2 * CO:3 * CO, 512:640].astype(BF)
 
+    pl.semaphore_wait(known.at[0], 8)
+    greet(known.at[1], around(2))
+
     def own_part(d):
         lo, hi = max(d, 1), min(d + 3, ND + 1)
         k0 = (lo - d) * KM
@@ -188,6 +187,10 @@
             tb[0:XROWS, at:at + ROWS] = flipped[e * XROWS:(e + 1) * XROWS]
             tb[XROWS:XROWS + CI, at:at + ROWS] = side[e * CI:(e + 1) * CI]
             tb[XROWS + CI:XROWS + 2 * CI, at:at + ROWS] = side[48 + e * CI:48 + (e + 1) * CI]
+
+    pl.semaphore_wait(known.at[1], 8)
+    far_apart = [(lax.rem(i + 4, nd), j), (lax.rem(i + nd - 4, nd), j)]
+    greet(known.at[2], far_apart)
 
     for copy in vol_copies:
         copy.wait_recv()
@@ -286,6 +289,7 @@
         here = full.at[own_piece]
         return remote(here, here, s_c.at[k], r_c.at[k], near_target(k)[1])
 
+    pl.semaphore_wait(known.at[2], 2)
     run(NEAR, scatter_copy, "start")
     rs[near] = comp[own_piece]
 
@@ -472,6 +476,7 @@
             dma((NEAR,)), dma((NEAR,)),
             dma((FAR,)), dma((FAR,)),
             dma((NEAR,)), dma((NEAR,)),
+            pltpu.SemaphoreType.REGULAR((3,)),
         ],
         compiler_params=pltpu.CompilerParams(
             collective_id=0, has_side_effects=True, vmem_limit_bytes=58 * 2**20),

time: 47.7 us -> 46.1 us (0.966)
  Pallas kernels: 46.9 us -> 45.3 us
    pallas_call x1, Pallas kernels: 44.4 us -> 42.8 us  [shards(): pl.pallas_call(functools.partial(kernel_body, nd, nh), out_shape=out_shap...]
where the time goes in v3:
time: 46.1 us; the launch traced here: 45.9 us
  Pallas kernels  45.3 us (98%)
  between operations  0.64 us (1%)
    pallas_call x1, Pallas kernels, shards(): pl.pallas_call(functools.partial(kernel_body, nd, nh), out_shape=out_shap...  42.8 us
    pallas_call x1, Pallas kernels, shards(): pl.pallas_call(hand_over, out_shape=out_shape, in_specs=[vmem] * 4, out_s...  2.47 us

profile of v3, /device:TPU:1, one launch (start us, length us, event | category | flops | bytes accessed | tf_op | source)
XLA Modules:
  0.0 45.9 jit_solution(8110808666016491510)
XLA Ops:
  0.6 42.8 %conv_step.1 = (bf16[32,1,32,128]{3,2,1,0:T(8,128)(2,1)}, bf16[16,16,8,256]{3,2,1,0:T(8,128)(2,1)}, f32[3,3,32,48]{3,2,1,0:T(8,128)}, f32[1,32]{1,0:T(1,128)}) custom-call(bf16[16,16,8,256]{3,2,1,0:T(8,128)(2,1)} %vol_in.1, bf16[3,96,48]{2,1,0:T(8,128)(2,1)} %bitcast.3, f32[1,32]{1,0:T(1,128)} %bitcast.4, bf16[32,8,4,128]{3,2,1,0:T(4,128)(2,1)} %cot_in.1), custom_call_target="tpu_custom_call" | custom-call | flops 10000000000 | bytes 3145728 | tf_op jit(solution)/shard_map/conv_step/pallas_call | solution.py:438
  43.4 2.5 %hand_over.1 = (bf16[32,1,32,128]{3,2,1,0:T(8,128)(2,1)}, bf16[16,16,8,256]{3,2,1,0:T(8,128)(2,1)}, f32[3,3,32,48]{3,2,1,0:T(8,128)}, f32[1,32]{1,0:T(1,128)}) custom-call(bf16[32,1,32,128]{3,2,1,0:T(8,128)(2,1)} %get-tuple-element.12.refs_0_, bf16[16,16,8,256]{3,2,1,0:T(8,128)(2,1)} %get-tuple-element.13.refs_1_, ...), custom_call_target="tpu_custom_call" | custom-call | tf_op jit(solution)/shard_map/hand_over/pallas_call | solution.py:486

commit v4 on v3

--- a/solution.py
+++ b/solution.py
@@ -50,9 +50,9 @@
     return jnp.where(iota(x.shape, 1) == x.shape[1] - 1, jnp.zeros_like(x), rolled)
 
 
-def kernel_body(nd, nh, vol_in, ker, bias, cot_in, pooled, gvol, gker, gbias,
+def kernel_body(nd, nh, vol_in, ker, bias, cot_in, pooled_out, gvol_out, gker, gbias,
                 vol, cot, xa, xh, ga, tm, th, tb, acc, bm, om, um, cells, hs, rh, rd, ps, rpool, ph, rp, rpc, pd, rpd, comp, rs, rs2, piece,
-                full, s_in, s_v, r_v, s_p, r_p, s_g, r_g, s_a, r_a, s_b, r_b, s_c, r_c, known):
+                full, pooled, gvol, s_in, s_o, s_v, r_v, s_p, r_p, s_g, r_g, s_a, r_a, s_b, r_b, s_c, r_c, known):
     i = lax.axis_index("depth")
     j = lax.axis_index("height")
     up_i, dn_i = lax.rem(i + 1, nd), lax.rem(i + nd - 1, nd)
@@ -212,7 +212,7 @@
         total = None
         for k in range(2):
             d = 2 * q + k
-            rim = dot(th[...], xh[pl.ds(d, 3)].reshape(3 * 128, W))
+            rim = dot(th[...], xh[d:d + 3].reshape(3 * 128, W))
             own = bm[d]
             before = jnp.concatenate([own[:CO] + rim[:CO], own[CO:ROWS - CO], own[ROWS - CO:] + rim[CO:]], axis=0)
             before = before + bias_rows
@@ -224,18 +224,25 @@
             total = part if total is None else total + part
         cells[q] = total
 
-    acc[...] = jnp.zeros_like(acc)
-
-    def stage(s, carry):
-        forward(2 * s)
-        forward(2 * s + 1)
+    def taps_grad(s):
         ds = [4 * s + k for k in range(4)]
         right = jnp.concatenate([ga[d, ROWS:2 * ROWS] for d in ds], axis=1)
-        acc[0:3 * KM] += dot_nt(jnp.concatenate([xa[pl.ds(d, 3)].reshape(3 * KM, W) for d in ds], axis=1), right)
-        acc[3 * KM:] += dot_nt(jnp.concatenate([xh[pl.ds(d, 3)].reshape(3 * 128, W) for d in ds], axis=1), right)
-        return carry
-
-    lax.fori_loop(0, ND // 4, stage, 0)
+        own = dot_nt(jnp.concatenate([xa[d:d + 3].reshape(3 * KM, W) for d in ds], axis=1), right)
+        rim = dot_nt(jnp.concatenate([xh[d:d + 3].reshape(3 * 128, W) for d in ds], axis=1), right)
+        if s == 0:
+            acc[0:3 * KM] = own
+            acc[3 * KM:] = rim
+        else:
+            acc[0:3 * KM] += own
+            acc[3 * KM:] += rim
+
+    stages = ND // 4
+    for s in range(stages + 1):
+        if s < stages:
+            forward(2 * s)
+            forward(2 * s + 1)
+        if s > 0:
+            taps_grad(s - 1)
 
     def run(count, make, act):
         def step(k, carry):
@@ -381,6 +388,8 @@
     run(nh, pool_copy, "wait_recv")
     for o in range(CO):
         pooled[o, 0] = rpool[:, o].reshape(4 * nh, 128)
+    stores = [pltpu.make_async_copy(pooled, pooled_out, s_o.at[4])]
+    stores[0].start()
 
     for copy in grad_copies:
         copy.wait_recv()
@@ -400,6 +409,10 @@
             out = out + edges(rpc[side, 0], rpc[side, 1], none)
             out = out + jnp.where(none, zero_slab, rpd[side]).astype(F32)
         gvol[:, d] = out.astype(BF).reshape(CI, NH, W)
+        if d % 4 == 3:
+            part = pl.ds(d - 3, 4)
+            stores.append(pltpu.make_async_copy(gvol.at[:, part], gvol_out.at[:, part], s_o.at[d // 4]))
+            stores[-1].start()
 
     run(NEAR, gather_copy, "wait_recv")
     norm = 1.0 / math.sqrt(float(ND * NH * W * nd * nh))
@@ -411,6 +424,8 @@
     gker[2, 2, :, 32:48] = turned[CO:2 * CO, 96:112]
     gbias[...] = final[96:97, 2 * CO:3 * CO]
 
+    for copy in stores:
+        copy.wait()
     for copy in vol_copies + grad_copies:
         copy.wait_send()
     run(nh, pool_copy, "wait_send")
@@ -439,7 +454,7 @@
         functools.partial(kernel_body, nd, nh),
         out_shape=out_shape,
         in_specs=[anywhere, vmem, vmem, anywhere],
-        out_specs=(vmem,) * 4,
+        out_specs=(anywhere, anywhere, vmem, vmem),
         scratch_shapes=[
             pltpu.VMEM((CI, ND, NH, W), BF),
             pltpu.VMEM((CO, PAIRS, 4, 128), BF),
@@ -469,7 +484,10 @@
             pltpu.VMEM((FAR, PIECE, 128), F32),
             pltpu.VMEM((PIECE, 128), F32),
             pltpu.VMEM((128, 128), F32),
+            pltpu.VMEM((CO, 1, 4 * nh, 128), BF),
+            pltpu.VMEM((CI, ND, NH, W), BF),
             dma((2,)),
+            dma((5,)),
             dma((8,)), dma((8,)),
             dma((nh,)), dma((nh,)),
             dma((12,)), dma((12,)),

time: 46.1 us -> 45 us (0.976)
  Pallas kernels: 45.3 us -> 44.2 us
    pallas_call x1, Pallas kernels: 42.8 us -> 41.7 us  [shards(): pl.pallas_call(functools.partial(kernel_body, nd, nh), out_shape=out_shap...]
where the time goes in v4:
time: 45 us; the launch traced here: 44.8 us
  Pallas kernels  44.2 us (98%)
  between operations  0.64 us (1%)
    pallas_call x1, Pallas kernels, shards(): pl.pallas_call(functools.partial(kernel_body, nd, nh), out_shape=out_shap...  41.7 us
    pallas_call x1, Pallas kernels, shards(): pl.pallas_call(hand_over, out_shape=out_shape, in_specs=[vmem] * 4, out_s...  2.47 us

profile of v4, /device:TPU:1, one launch (start us, length us, event | category | flops | bytes accessed | tf_op | source)
XLA Modules:
  0.0 44.8 jit_solution(11976169843085788699)
XLA Ops:
  0.6 41.7 %conv_step.1 = (bf16[32,1,32,128]{3,2,1,0:T(8,128)(2,1)}, bf16[16,16,8,256]{3,2,1,0:T(8,128)(2,1)}, f32[3,3,32,48]{3,2,1,0:T(8,128)}, f32[1,32]{1,0:T(1,128)}) custom-call(bf16[16,16,8,256]{3,2,1,0:T(8,128)(2,1)} %vol_in.1, bf16[3,96,48]{2,1,0:T(8,128)(2,1)} %bitcast.3, f32[1,32]{1,0:T(1,128)} %bitcast.4, bf16[32,8,4,128]{3,2,1,0:T(4,128)(2,1)} %cot_in.1), custom_call_target="tpu_custom_call" | custom-call | flops 10000000000 | bytes 3145728 | tf_op jit(solution)/shard_map/conv_step/pallas_call | solution.py:453
  42.3 2.5 %hand_over.1 = (bf16[32,1,32,128]{3,2,1,0:T(8,128)(2,1)}, bf16[16,16,8,256]{3,2,1,0:T(8,128)(2,1)}, f32[3,3,32,48]{3,2,1,0:T(8,128)}, f32[1,32]{1,0:T(1,128)}) custom-call(bf16[32,1,32,128]{3,2,1,0:T(8,128)(2,1)} %get-tuple-element.12.refs_0_, bf16[16,16,8,256]{3,2,1,0:T(8,128)(2,1)} %get-tuple-element.13.refs_1_, ...), custom_call_target="tpu_custom_call" | custom-call | tf_op jit(solution)/shard_map/hand_over/pallas_call | solution.py:504

commit v5 on v4

--- a/solution.py
+++ b/solution.py
@@ -48,6 +48,14 @@
 def shift_left(x):
     rolled = pltpu.roll(x, x.shape[1] - 1, 1)
     return jnp.where(iota(x.shape, 1) == x.shape[1] - 1, jnp.zeros_like(x), rolled)
+
+
+def in_fours(count, body):
+    def step(n, carry):
+        for k in range(4):
+            body(4 * n + k)
+        return carry
+    lax.fori_loop(0, count // 4, step, 0)
 
 
 def kernel_body(nd, nh, vol_in, ker, bias, cot_in, pooled_out, gvol_out, gker, gbias,
@@ -300,19 +308,31 @@
     run(NEAR, scatter_copy, "start")
     rs[near] = comp[own_piece]
 
-    for q in range(PAIRS):
+    def pool(q):
         total = cells[q]
         high = total.astype(BF)
         low = (total - high.astype(F32)).astype(BF)
         mean = dot(jnp.concatenate([high, low], axis=1), gather).astype(BF)
         ps[q] = dot(to_o_major, mean).astype(BF).reshape(CO, 4, 128)
+
+    in_fours(PAIRS, pool)
     run(nh, pool_copy, "start")
     rpool[j] = ps[j]
 
-    for d in range(ND):
+    def widen(d):
         g = ga[d, ROWS:2 * ROWS]
         ga[d, 0:ROWS] = shift_left(g)
         ga[d, 2 * ROWS:3 * ROWS] = shift_right(g)
+
+    in_fours(ND, widen)
+
+    run(NEAR, scatter_copy, "wait_recv")
+    total = rs[0]
+    for k in range(1, NEAR):
+        total = total + rs[k]
+    piece[...] = total
+    rs2[far] = total
+    run(FAR, all_copy, "start")
 
     def back(d):
         lo, hi = max(d - 1, 0), min(d + 2, ND)
@@ -351,14 +371,6 @@
         out = back(d)
         om[d] = out[:XROWS]
         keep(d, out)
-
-    run(NEAR, scatter_copy, "wait_recv")
-    total = rs[0]
-    for k in range(1, NEAR):
-        total = total + rs[k]
-    piece[...] = total
-    rs2[far] = total
-    run(FAR, all_copy, "start")
 
     def inner(d0, count):
         def step(n, carry):

time: 45 us -> 44.7 us (level)
  no operation moved by 1% of the time
where the time goes in v5:
time: 44.7 us; the launch traced here: 44.5 us
  Pallas kernels  43.9 us (98%)
  between operations  0.64 us (1%)
    pallas_call x1, Pallas kernels, shards(): pl.pallas_call(functools.partial(kernel_body, nd, nh), out_shape=out_shap...  41.4 us
    pallas_call x1, Pallas kernels, shards(): pl.pallas_call(hand_over, out_shape=out_shape, in_specs=[vmem] * 4, out_s...  2.47 us

profile of v5, /device:TPU:1, one launch (start us, length us, event | category | flops | bytes accessed | tf_op | source)
XLA Modules:
  0.0 44.5 jit_solution(12301564005168919753)
XLA Ops:
  0.6 41.4 %conv_step.1 = (bf16[32,1,32,128]{3,2,1,0:T(8,128)(2,1)}, bf16[16,16,8,256]{3,2,1,0:T(8,128)(2,1)}, f32[3,3,32,48]{3,2,1,0:T(8,128)}, f32[1,32]{1,0:T(1,128)}) custom-call(bf16[16,16,8,256]{3,2,1,0:T(8,128)(2,1)} %vol_in.1, bf16[3,96,48]{2,1,0:T(8,128)(2,1)} %bitcast.3, f32[1,32]{1,0:T(1,128)} %bitcast.4, bf16[32,8,4,128]{3,2,1,0:T(4,128)(2,1)} %cot_in.1), custom_call_target="tpu_custom_call" | custom-call | flops 10000000000 | bytes 3145728 | tf_op jit(solution)/shard_map/conv_step/pallas_call | solution.py:465
  42.1 2.5 %hand_over.1 = (bf16[32,1,32,128]{3,2,1,0:T(8,128)(2,1)}, bf16[16,16,8,256]{3,2,1,0:T(8,128)(2,1)}, f32[3,3,32,48]{3,2,1,0:T(8,128)}, f32[1,32]{1,0:T(1,128)}) custom-call(bf16[32,1,32,128]{3,2,1,0:T(8,128)(2,1)} %get-tuple-element.12.refs_0_, bf16[16,16,8,256]{3,2,1,0:T(8,128)(2,1)} %get-tuple-element.13.refs_1_, ...), custom_call_target="tpu_custom_call" | custom-call | tf_op jit(solution)/shard_map/hand_over/pallas_call | solution.py:516
